TPU v7x, 32 devices: a whole 2x2x4 slice. The times are simulated.
32 devices in a mesh: groups: 2 (over x), seg: 8 (over z, y), head: 2 (over core).
Axes of the slice: x: 2, y: 2, z: 4, core: 2. Of those that a mesh axis runs over, the one named last changes fastest.
Arguments:
- features: bfloat16 [32768, 128], P(('groups', 'seg', 'head')), parts along dimension 0, may hold values from -6 to 6
- positions: int32 [32768], P(('groups', 'seg', 'head')), parts along dimension 0, may hold values from 0 to 16383, as said below
- neighbors: int32 [32768, 27], P(('groups', 'seg', 'head')), parts along dimension 0, may hold values from -1 to 1535, as said below
- send_rows: int32 [128, 128], P(('groups', 'seg', 'head')), parts along dimension 0, may hold values from -1 to 1023, as said below
- conv_weight: bfloat16 [27, 128, 128], replicated, may hold values from -0.15625 to 0.15625
- conv_bias: float32 [128], replicated, may hold values from -1.75 to 1.75
- cpe_weight: bfloat16 [128, 128], replicated, may hold values from -0.5 to 0.5
- cpe_bias: float32 [128], replicated, may hold values from -3 to 3
- norm_gain: float32 [3, 128], replicated, may hold values from 0.5 to 1.5
- norm_bias: float32 [3, 128], replicated, may hold values from -1.75 to 1.75
- qkv_weight: bfloat16 [128, 384], replicated
- qkv_bias: float32 [384], replicated, may hold values from -1.75 to 1.75
- proj_weight: bfloat16 [128, 128], replicated, may hold values from -0.5 to 0.5
- proj_bias: float32 [128], replicated, may hold values from -1.75 to 1.75
- fc1_weight: bfloat16 [128, 512], replicated, may hold values from -0.5 to 0.5
- fc1_bias: float32 [512], replicated, may hold values from -1.75 to 1.75
- fc2_weight: bfloat16 [512, 128], replicated, may hold values from -0.25 to 0.25
- fc2_bias: float32 [128], replicated, may hold values from -1.75 to 1.75
Outputs:
- block_out: bfloat16 [32768, 128], P(('groups', 'seg', 'head')), parts along dimension 0
There are 2 independent parts, one for each index of `groups`. A program takes and returns all parts, laid end to end along the dimension named above; an argument that names none is the same for every part. Nothing has to cross between parts.
Inputs may be any that keep to these rules, and one draw needn't show every extreme that they name: `positions`: A permutation of the points. Points come in aligned runs of 16 consecutive z-order points that go to 16 consecutive places starting at a multiple of 16. The points of device d go only to the ranges of 1024 places of devices (d + s) mod 16 with s from -7 to 8, at most 128 places in the range of any one device, and every device sends exactly 128 to some device in every draw. `neighbors`: entry k = 13 of each row names the point itself. The coding of the other entries is that of the step neighbor_rows; every halo value names an entry t below the number of live entries of its list when that list's device exists. `send_rows`: row 4 * e + j lists distinct rows of device e that device e + b_j reads, b = (1, 2, -1, -2), followed by -1; each list holds 1 to 128 rows, and some list holds 128 in every draw.
All inputs are finite; a program needn't handle non-finite values.
Results may differ from a plain program's by a relative error of at most 0.007.
The roundings to bfloat16 on the way count: a program that leaves them out, or rounds other values in their place, can miss the bound.
Values may be sent and summed in bfloat16 or wider, within the bound.
A program may use at most 64 MiB of HBM per device.

v0:
```python
import math

import jax
import jax.numpy as jnp
from jax import lax
from jax.sharding import PartitionSpec as P

HEADS = 8
PATCH = 1024


norm_epsilon = 1e-05
halo_offsets = (1, 2, -1, -2)


def passed_along(block, axis, distance):
    devices = range(lax.axis_size(axis))
    route = [(i - distance, i) for i in devices if i - distance in devices]
    return lax.ppermute(block, axis, route)


def normalize(values, norm_scale, norm_shift):
    row_mean = jnp.mean(values, axis=-1, keepdims=True)
    centred = values - row_mean
    spread = jnp.mean(centred * centred, axis=-1, keepdims=True)
    return centred * lax.rsqrt(spread + norm_epsilon) * norm_scale + norm_shift


def project_rows(source_rows, norm_scale, norm_shift, weight, bias):
    normed = normalize(source_rows.astype(jnp.float32), norm_scale, norm_shift).astype(jnp.bfloat16)
    return (jnp.dot(normed, weight, preferred_element_type=jnp.float32) + bias).astype(jnp.bfloat16)


def attend_patch(patch_qkv, channels):
    head_width = channels // HEADS
    scale = head_width ** (-0.5)

    def split_heads(columns):
        return columns.reshape(PATCH, HEADS, head_width).transpose(1, 0, 2)

    queries = split_heads(patch_qkv[:, :channels])
    keys_all = split_heads(patch_qkv[:, channels : 2 * channels])
    values_all = split_heads(patch_qkv[:, 2 * channels :])

    def one_head(head_item):
        query, key_rows, value_rows = head_item
        scores = (
            lax.dot_general(
                query, key_rows, (((1,), (1,)), ((), ())), preferred_element_type=jnp.float32
            )
            * scale
        )
        row_max = jnp.max(scores, axis=-1, keepdims=True)
        exp_scores = jnp.exp(scores - row_max)
        weights = (exp_scores / jnp.sum(exp_scores, axis=-1, keepdims=True)).astype(jnp.bfloat16)
        return jnp.dot(weights, value_rows, preferred_element_type=jnp.float32).astype(jnp.bfloat16)

    head_out = lax.map(one_head, (queries, keys_all, values_all))
    return head_out.transpose(1, 0, 2).reshape(PATCH, channels)


def fill_buckets(labels, label_count, unit_rows, capacity, lifted, positions):
    row_count, channels = lifted.shape
    unit_count = row_count // unit_rows
    per_label = capacity // unit_rows
    owners = jnp.arange(label_count, dtype=jnp.int32)
    marks = (labels[:, None] == owners[None, :]).astype(jnp.int32)
    earlier = jnp.cumsum(marks, axis=0) - marks
    unit_rank = jnp.sum(earlier * marks, axis=1)
    unit_slot = labels * per_label + unit_rank
    slot_total = label_count * per_label
    matches = jnp.arange(slot_total, dtype=jnp.int32)[:, None] == unit_slot[None, :]
    unit_values = lifted.reshape(unit_count, unit_rows * channels)
    bucket = jnp.dot(
        matches.astype(jnp.bfloat16), unit_values, preferred_element_type=jnp.float32
    ).astype(jnp.bfloat16)
    bucket = bucket.reshape(label_count, capacity, channels)
    unit_place = positions.reshape(unit_count, unit_rows)[:, 0]
    first_places = jnp.sum(jnp.where(matches, unit_place[None, :], 0), axis=1)
    is_filled = jnp.any(matches, axis=1)
    slot_places = first_places[:, None] + jnp.arange(unit_rows, dtype=jnp.int32)[None, :]
    bucket_places = jnp.where(is_filled[:, None], slot_places, -1).reshape(label_count, capacity)
    return (bucket, bucket_places)


def per_device(
    features,
    positions,
    neighbors,
    send_rows,
    conv_weight,
    conv_bias,
    cpe_weight,
    cpe_bias,
    norm_gain,
    norm_bias,
    qkv_weight,
    qkv_bias,
    proj_weight,
    proj_bias,
    fc1_weight,
    fc1_bias,
    fc2_weight,
    fc2_bias,
):
    row_count, channels = features.shape
    devices = lax.axis_size(("seg", "head"))
    my_index = lax.axis_index(("seg", "head"))
    row_iota = jnp.arange(row_count, dtype=jnp.int32)
    table_parts = [features]
    for direction, offset in enumerate(halo_offsets):
        picks = send_rows[direction]
        pick_table = (picks[:, None] == row_iota[None, :]).astype(jnp.bfloat16)
        outgoing = jnp.dot(pick_table, features, preferred_element_type=jnp.float32).astype(
            jnp.bfloat16
        )
        table_parts.append(passed_along(outgoing, ("seg", "head"), offset))
    table_parts.append(jnp.zeros((1, channels), features.dtype))
    row_table = jnp.concatenate(table_parts, axis=0)
    empty_row = row_table.shape[0] - 1
    kernel = neighbors.shape[1]
    flat_weight = conv_weight.reshape(kernel * channels, channels)
    block_rows = math.gcd(row_count, 512)

    def conv_block(block_ids):
        safe_ids = jnp.where(block_ids >= 0, block_ids, empty_row)
        gathered = row_table[safe_ids]
        conv_part = (
            jnp.dot(
                gathered.reshape(block_ids.shape[0], kernel * channels),
                flat_weight,
                preferred_element_type=jnp.float32,
            )
            + conv_bias
        )
        return (
            jnp.dot(conv_part.astype(jnp.bfloat16), cpe_weight, preferred_element_type=jnp.float32)
            + cpe_bias
        )

    encoded = lax.map(
        conv_block, neighbors.reshape(row_count // block_rows, block_rows, kernel)
    ).reshape(row_count, channels)
    lifted = (features.astype(jnp.float32) + normalize(encoded, norm_gain[0], norm_bias[0])).astype(
        jnp.bfloat16
    )
    unit_rows = row_count // 64
    capacity = 8 * unit_rows
    unit_dest = positions[::unit_rows] // row_count
    first_place = my_index * row_count
    local_units = row_count // unit_rows
    bucket, bucket_places = fill_buckets(unit_dest, devices, unit_rows, capacity, lifted, positions)
    arrived_rows, arrived_places = (
        lax.all_to_all(bucket, ("seg", "head"), split_axis=0, concat_axis=0, tiled=True),
        lax.all_to_all(bucket_places, ("seg", "head"), split_axis=0, concat_axis=0, tiled=True),
    )
    width = arrived_rows.shape[-1]
    flat_places = arrived_places.reshape(-1)
    arrived_units = flat_places.shape[0] // unit_rows
    unit_place = flat_places.reshape(arrived_units, unit_rows)[:, 0]
    unit_target = jnp.where(unit_place >= 0, (unit_place - first_place) // unit_rows, -1)
    matches = (jnp.arange(local_units, dtype=jnp.int32)[:, None] == unit_target[None, :]).astype(
        jnp.bfloat16
    )
    unit_values = arrived_rows.reshape(arrived_units, unit_rows * width)
    placed = jnp.dot(matches, unit_values, preferred_element_type=jnp.float32).astype(
        arrived_rows.dtype
    )
    arranged = placed.reshape(row_count, width)
    joined_qkv = project_rows(arranged, norm_gain[1], norm_bias[1], qkv_weight, qkv_bias)

    def patch_attention(patch_qkv):
        return attend_patch(patch_qkv, channels)

    attended = lax.map(
        patch_attention, joined_qkv.reshape(row_count // PATCH, PATCH, 3 * channels)
    ).reshape(row_count, channels)
    residual_mid = (
        arranged.astype(jnp.float32)
        + jnp.dot(attended, proj_weight, preferred_element_type=jnp.float32)
        + proj_bias
    )
    normed_mid = normalize(residual_mid, norm_gain[2], norm_bias[2]).astype(jnp.bfloat16)
    hidden = jax.nn.gelu(
        jnp.dot(normed_mid, fc1_weight, preferred_element_type=jnp.float32) + fc1_bias,
        approximate=False,
    ).astype(jnp.bfloat16)
    return (
        residual_mid + jnp.dot(hidden, fc2_weight, preferred_element_type=jnp.float32) + fc2_bias
    ).astype(jnp.bfloat16)


def solution(mesh):
    placed = (
        P(("groups", "seg", "head"), None),
        P(("groups", "seg", "head")),
        P(("groups", "seg", "head"), None),
        P(("groups", "seg", "head"), None),
        P(),
        P(),
        P(),
        P(),
        P(),
        P(),
        P(),
        P(),
        P(),
        P(),
        P(),
        P(),
        P(),
        P(),
    )
    return jax.shard_map(
        per_device,
        mesh=mesh,
        in_specs=placed,
        out_specs=P(("groups", "seg", "head"), None),
        check_vma=False,
    )
```

profile of v0, /device:TPU:0, one launch (start us, length us, event | category | flops | bytes accessed | tf_op | source)
XLA Modules:
  0.0 159.7 jit_solution(9386924253785348584)
XLA Ops:
  0.0 0.8 slice_bitcast_fusion.6
  0.9 1.2 convolution_convert_fusion.5
  2.1 2.4 %collective-permute-start = (bf16[128,128]{1,0:T(8,128)(2,1)S(1)}, bf16[128,128]{1,0:T(8,128)(2,1)S(1)}, u32[]{:S(2)}, u32[]{:S(2)}) collective-permute-start(bf16[128,128]{1,0:T(8,128)(2,1)S(1)} %convolution_convert_fusion.5), channel_id=1, source_target_pairs={{0,1},{1,2},{2,3},{3,4},{4,5},{5,6},{6,7},{7,8},{8,9},{9,10},{10,1... | collective-permute-start | bytes 98312 | tf_op jit(solution)/shard_map/ppermute | solution.py:19
  4.5 1.2 convolution_convert_fusion.4
  5.7 4.4 %collective-permute-start.1 = (bf16[128,128]{1,0:T(8,128)(2,1)S(1)}, bf16[128,128]{1,0:T(8,128)(2,1)S(1)}, u32[]{:S(2)}, u32[]{:S(2)}) collective-permute-start(bf16[128,128]{1,0:T(8,128)(2,1)S(1)} %convolution_convert_fusion.4), channel_id=1, source_target_pairs={{0,2},{1,3},{2,4},{3,5},{4,6},{5,7},{6,8},{7,9},{8,10},{9,11},{10,... | collective-permute-start | bytes 98312 | tf_op jit(solution)/shard_map/ppermute | solution.py:19
  10.1 1.2 convolution_convert_fusion.3
  11.4 1.3 collective-permute-start.2
  12.7 1.2 convolution_convert_fusion.2
  13.9 1.3 collective-permute-start.3
  15.2 0.8 slice.51
  18.8 10.0 %all-to-all-start = ((s32[16,1,128]{2,1,0:T(1,128)}), s32[16,1,128]{2,1,0:T(1,128)S(1)}, u32[]{:S(2)}, u32[]{:S(2)}) async-start(s32[16,1,128]{2,1,0:T(1,128)} %bitcast.6), calls=%async_computation | async-start | bytes 16384 | tf_op jit(solution)/shard_map/all_to_all | solution.py:155
  30.0 78.9 %while.27 = (s32[]{:T(128)}, f32[2,512,128]{2,1,0:T(8,128)S(1)}, s32[2,512,27]{2,1,0:T(8,128)S(1)}, bf16[1537,128]{1,0:T(8,128)(2,1)S(1)}, bf16[3456,128]{1,0:T(...) while((s32[]{:T(128)}, f32[2,512,128]{2,1,0:T(8,128)S(1)}, ...), condition=%wide.region_5.6_spmd, body=%wide.region_4.5_spmd.sunk | while | flops 470042112 | bytes 19264612 | solution.py:141
  30.3 28.4 %gather_fusion = bf16[13824,128]{1,0:T(8,128)(2,1)} fusion(bf16[1537,128]{1,0:T(8,128)(2,1)S(1)} %get-tuple-element.238, s32[14336]{0:T(1024)S(1)} %pad_clamp_fusion.2), kind=kCustom, calls=%fused_computation.clone.1 | custom fusion | bytes 7133184 | tf_op jit(solution)/shard_map/while/body/eval_jaxpr/gather | solution.py:127
  58.7 7.6 %reshape.279 = bf16[512,3456]{1,0:T(8,128)(2,1)} reshape(bf16[13824,128]{1,0:T(8,128)(2,1)} %gather_fusion) | data formatting | bytes 7077888 | tf_op jit(solution)/shard_map/while/body/eval_jaxpr/reshape | solution.py:130
  66.3 3.2 %fusion.149 = f32[2,512,128]{2,1,0:T(8,128)S(1)} fusion(f32[2,512,128]{2,1,0:T(8,128)S(1)} %get-tuple-element.227, s32[]{:T(128)} %get-tuple-element.226, bf16[128,128]{1,0:T(8,128)(2,1)S(1)} %get-tuple-element.241, bf16[512,3456]{1,0:T(8,128)(2,1)} %reshape.279, bf16[3456,128]{1,0:T(8,128)(2,1)S(1)} %get-tuple-element.239, ...), kind=kOutput, calls=%fused_computation.21.clone.1 | convolution fusion | flops 469958656 | bytes 4719620 | tf_op jit(solution)/shard_map/while/body/eval_jaxpr/dot_general | solution.py:137
  69.8 28.4 %gather_fusion = bf16[13824,128]{1,0:T(8,128)(2,1)} fusion(bf16[1537,128]{1,0:T(8,128)(2,1)S(1)} %get-tuple-element.238, s32[14336]{0:T(1024)S(1)} %pad_clamp_fusion.2), kind=kCustom, calls=%fused_computation.clone.1 | custom fusion | bytes 7133184 | tf_op jit(solution)/shard_map/while/body/eval_jaxpr/gather | solution.py:127
  98.2 7.6 %reshape.279 = bf16[512,3456]{1,0:T(8,128)(2,1)} reshape(bf16[13824,128]{1,0:T(8,128)(2,1)} %gather_fusion) | data formatting | bytes 7077888 | tf_op jit(solution)/shard_map/while/body/eval_jaxpr/reshape | solution.py:130
  105.7 3.2 %fusion.149 = f32[2,512,128]{2,1,0:T(8,128)S(1)} fusion(f32[2,512,128]{2,1,0:T(8,128)S(1)} %get-tuple-element.227, s32[]{:T(128)} %get-tuple-element.226, bf16[128,128]{1,0:T(8,128)(2,1)S(1)} %get-tuple-element.241, bf16[512,3456]{1,0:T(8,128)(2,1)} %reshape.279, bf16[3456,128]{1,0:T(8,128)(2,1)S(1)} %get-tuple-element.239, ...), kind=kOutput, calls=%fused_computation.21.clone.1 | convolution fusion | flops 469958656 | bytes 4719620 | tf_op jit(solution)/shard_map/while/body/eval_jaxpr/dot_general | solution.py:137
  110.5 1.0 reshape.243
  111.5 6.0 %all-to-all-start.1 = ((bf16[16,128,128]{2,1,0:T(8,128)(2,1)}), bf16[16,128,128]{2,1,0:T(8,128)(2,1)S(1)}, u32[]{:S(2)}, u32[]{:S(2)}) async-start(bf16[16,128,128]{2,1,0:T(8,128)(2,1)} %reshape.243), calls=%async_computation.1 | async-start | bytes 1048576 | tf_op jit(solution)/shard_map/all_to_all | solution.py:154
  119.1 12.9 %all-to-all-done.1 = bf16[16,128,128]{2,1,0:T(8,128)(2,1)S(1)} async-done(((bf16[16,128,128]{2,1,0:T(8,128)(2,1)}), bf16[16,128,128]{2,1,0:T(8,128)(2,1)S(1)}, u32[]{:S(2)}, u32[]{:S(2)}) %all-to-all-start.1) | async-done | bytes 524320 | tf_op jit(solution)/shard_map/all_to_all | solution.py:154
  134.2 19.0 %while.28 = (s32[]{:T(128)}, bf16[8,1024,16]{1,2,0:T(8,128)(2,1)S(1)}, bf16[8,1024,16]{1,2,0:T(8,128)(2,1)S(1)}, bf16[8,1024,16]{1,2,0:T(8,128)(2,1)S(1)}, bf16[8,1024,16]{1,2,0:T(8,128)(2,1)S(1)}, /*index=5*/s32[]{:T(128)}) while((s32[]{:T(128)}, bf16[8,1024,16]{1,2,0:T(8,128)(2,1)S(1)}, bf16[8,1024,16]{1,2,0:T(8,128)(2,1)S(1)}, ...), condition=%wide.region_13.14_spmd, body=%wide.region_10.13_spmd.sunk | while | flops 76560384 | bytes 12736581 | solution.py:58
  135.7 0.9 fusion.152
  138.1 0.9 fusion.152
  140.4 0.9 fusion.152
  142.8 0.9 fusion.152
  145.2 0.9 fusion.152
  147.5 0.9 fusion.152
  149.9 0.9 fusion.152
  152.3 0.9 fusion.152
  153.6 5.3 %fusion.34 = bf16[1024,128]{0,1:T(8,128)(2,1)S(1)} fusion(f32[1024,128]{0,1:T(8,128)S(1)} %get-tuple-element.129, bf16[512,128]{1,0:T(8,128)(2,1)S(1)} %copy-done, bf16[128,512]{1,0:T(8,128)(2,1)S(1)} %copy-done.8, f32[512]{0:T(512)S(1)} %copy-done.10, f32[128]{0:T(128)S(1)} %copy-done.13, f32[128]{0:T(128)S(1)} %get-tuple-element.121, ...), kind=kOutput, calls=%fused_computation.56 | convolution fusion | flops 304087040 | bytes 1060352 | tf_op jit(solution)/shard_map/dot_general | solution.py:189
  158.9 0.8 copy.43
  (112 shorter events, 21.7 us)
Async XLA Ops:
  0.0 153.5 %copy-start = (bf16[512,128]{1,0:T(8,128)(2,1)S(1)}, bf16[512,128]{1,0:T(8,128)(2,1)}, u32[]{:S(2)}) copy-start(bf16[512,128]{1,0:T(8,128)(2,1)} %param.38) | copy-start | bytes 393220
  0.0 29.6 %copy-start.1 = (bf16[1024,128]{1,0:T(8,128)(2,1)S(1)}, bf16[1024,128]{1,0:T(8,128)(2,1)}, u32[]{:S(2)}) copy-start(bf16[1024,128]{1,0:T(8,128)(2,1)} %param.22) | copy-start | bytes 786436
  0.0 29.6 %copy-start.2 = (s32[1024,27]{0,1:T(8,128)S(1)}, s32[1024,27]{0,1:T(8,128)}, u32[]{:S(2)}) copy-start(s32[1024,27]{0,1:T(8,128)} %param.24) | copy-start | bytes 331780
  0.0 30.0 %copy-start.7 = (bf16[27,128,128]{2,1,0:T(8,128)(2,1)S(1)}, bf16[27,128,128]{2,1,0:T(8,128)(2,1)}, u32[]{:S(2)}) copy-start(bf16[27,128,128]{2,1,0:T(8,128)(2,1)} %param.26) | copy-start | bytes 2654212
  0.0 30.0 %copy-start.11 = (f32[128]{0:T(128)S(1)}, f32[128]{0:T(128)}, u32[]{:S(2)}) copy-start(f32[128]{0:T(128)} %param.27) | copy-start | bytes 1540
  0.0 30.0 %copy-start.9 = (bf16[128,128]{1,0:T(8,128)(2,1)S(1)}, bf16[128,128]{1,0:T(8,128)(2,1)}, u32[]{:S(2)}) copy-start(bf16[128,128]{1,0:T(8,128)(2,1)} %param.28) | copy-start | bytes 98308
  0.0 30.0 %copy-start.12 = (f32[128]{0:T(128)S(1)}, f32[128]{0:T(128)}, u32[]{:S(2)}) copy-start(f32[128]{0:T(128)} %param.29) | copy-start | bytes 1540
  2.1 27.8 %collective-permute-start = (bf16[128,128]{1,0:T(8,128)(2,1)S(1)}, bf16[128,128]{1,0:T(8,128)(2,1)S(1)}, u32[]{:S(2)}, u32[]{:S(2)}) collective-permute-start(bf16[128,128]{1,0:T(8,128)(2,1)S(1)} %convolution_convert_fusion.5), channel_id=1, source_target_pairs={{0,1},{1,2},{2,3},{3,4},{4,5},{5,6},{6,7},{7,8},{8,9},{9,10},{10,1... | collective-permute-start | bytes 98312 | tf_op jit(solution)/shard_map/ppermute | solution.py:19
  5.7 24.2 %collective-permute-start.1 = (bf16[128,128]{1,0:T(8,128)(2,1)S(1)}, bf16[128,128]{1,0:T(8,128)(2,1)S(1)}, u32[]{:S(2)}, u32[]{:S(2)}) collective-permute-start(bf16[128,128]{1,0:T(8,128)(2,1)S(1)} %convolution_convert_fusion.4), channel_id=1, source_target_pairs={{0,2},{1,3},{2,4},{3,5},{4,6},{5,7},{6,8},{7,9},{8,10},{9,11},{10,... | collective-permute-start | bytes 98312 | tf_op jit(solution)/shard_map/ppermute | solution.py:19
  11.4 18.6 %collective-permute-start.2 = (bf16[128,128]{1,0:T(8,128)(2,1)S(1)}, bf16[128,128]{1,0:T(8,128)(2,1)S(1)}, u32[]{:S(2)}, u32[]{:S(2)}) collective-permute-start(bf16[128,128]{1,0:T(8,128)(2,1)S(1)} %convolution_convert_fusion.3), channel_id=1, source_target_pairs={{1,0},{2,1},{3,2},{4,3},{5,4},{6,5},{7,6},{8,7},{9,8},{10,9},{11,1... | collective-permute-start | bytes 98312 | tf_op jit(solution)/shard_map/ppermute | solution.py:19
  13.9 16.0 %collective-permute-start.3 = (bf16[128,128]{1,0:T(8,128)(2,1)S(1)}, bf16[128,128]{1,0:T(8,128)(2,1)S(1)}, u32[]{:S(2)}, u32[]{:S(2)}) collective-permute-start(bf16[128,128]{1,0:T(8,128)(2,1)S(1)} %convolution_convert_fusion.2), channel_id=1, source_target_pairs={{2,0},{3,1},{4,2},{5,3},{6,4},{7,5},{8,6},{9,7},{10,8},{11,9},{12,... | collective-permute-start | bytes 98312 | tf_op jit(solution)/shard_map/ppermute | solution.py:19
  18.8 92.7 %all-to-all-start = ((s32[16,1,128]{2,1,0:T(1,128)}), s32[16,1,128]{2,1,0:T(1,128)S(1)}, u32[]{:S(2)}, u32[]{:S(2)}) async-start(s32[16,1,128]{2,1,0:T(1,128)} %bitcast.6), calls=%async_computation | async-start | bytes 16384 | tf_op jit(solution)/shard_map/all_to_all | solution.py:155
  111.5 20.5 %all-to-all-start.1 = ((bf16[16,128,128]{2,1,0:T(8,128)(2,1)}), bf16[16,128,128]{2,1,0:T(8,128)(2,1)S(1)}, u32[]{:S(2)}, u32[]{:S(2)}) async-start(bf16[16,128,128]{2,1,0:T(8,128)(2,1)} %reshape.243), calls=%async_computation.1 | async-start | bytes 1048576 | tf_op jit(solution)/shard_map/all_to_all | solution.py:154
  132.2 1.2 copy-start.3
  132.2 1.1 copy-start.5
  134.1 19.0 %copy-start.4 = (bf16[128,128]{1,0:T(8,128)(2,1)S(1)}, bf16[128,128]{1,0:T(8,128)(2,1)}, u32[]{:S(2)}) copy-start(bf16[128,128]{1,0:T(8,128)(2,1)} %param.34) | copy-start | bytes 98308
  134.1 19.0 %copy-start.6 = (f32[128]{0:T(128)S(1)}, f32[128]{0:T(128)}, u32[]{:S(2)}) copy-start(f32[128]{0:T(128)} %param.35) | copy-start | bytes 1540
  134.1 19.4 %copy-start.8 = (bf16[128,512]{1,0:T(8,128)(2,1)S(1)}, bf16[128,512]{1,0:T(8,128)(2,1)}, u32[]{:S(2)}) copy-start(bf16[128,512]{1,0:T(8,128)(2,1)} %param.36) | copy-start | bytes 393220
  134.2 19.4 %copy-start.10 = (f32[512]{0:T(512)S(1)}, f32[512]{0:T(512)}, u32[]{:S(2)}) copy-start(f32[512]{0:T(512)} %param.37) | copy-start | bytes 6148
  134.2 19.4 %copy-start.13 = (f32[128]{0:T(128)S(1)}, f32[128]{0:T(128)}, u32[]{:S(2)}) copy-start(f32[128]{0:T(128)} %param.39) | copy-start | bytes 1540
where the time goes:
time: 161 us; the launch traced here: 160 us
  local copies, waits for them, and re-layouts  79.7 us (50%)
  matrix products  31.3 us (19%)
  starting transfers between devices  25.4 us (16%)
  waiting for transfers between devices  12.9 us (8%)
  other arithmetic  9.65 us (6%)
    gather x2, local copies, waits for them, and re-layouts, conv_block(): gathered = row_table[safe_ids]  56.7 us
    reshape x2, local copies, waits for them, and re-layouts, conv_block(): gathered.reshape(block_ids.shape[0], kernel * channels)  15.1 us
    all_to_all x1, waiting for transfers between devices, per_device(): lax.all_to_all(bucket, ('seg', 'head'), split_axis=0, concat_axis=0, tile...  12.9 us
    all_to_all x1, starting transfers between devices, per_device(): lax.all_to_all(bucket_places, ('seg', 'head'), split_axis=0, concat_axis=...  10 us
    ppermute x4, starting transfers between devices, passed_along(): return lax.ppermute(block, axis, route)  9.39 us
    dot_general x8, matrix products, one_head(): jnp.dot(weights, value_rows, preferred_element_type=jnp.float32)  6.96 us
    dot_general x2, matrix products, conv_block(): jnp.dot(conv_part.astype(jnp.bfloat16), cpe_weight, preferred_element_typ...  6.45 us
    dot_general x8, matrix products, one_head(): lax.dot_general(query, key_rows, (((1,), (1,)), ((), ())), preferred_elem...  6.08 us
  transfers between devices with their start and end apart: 6, of which 1 were waited for; matrix products, arithmetic and copies ran while one was open for 57% of the time, Pallas kernels for 0%

commit v1 on v0

v1 whole, which is shorter than its diff:
```python
import functools
import math

import jax
import jax.numpy as jnp
from jax import lax
from jax.experimental import pallas as pl
from jax.experimental.pallas import tpu as pltpu
from jax.sharding import PartitionSpec as P

HEADS = 8
PEERS = 16
BACK = 7
UNITS_PER_PEER = 8
UNIT = 16

norm_epsilon = 1e-05
halo_offsets = (1, 2, -1, -2)
MESH = pl.DeviceIdType.MESH
VM = pl.BlockSpec(memory_space=pltpu.VMEM)
SM = pl.BlockSpec(memory_space=pltpu.SMEM)
f32 = jnp.float32
bf16 = jnp.bfloat16


def normalize(values, norm_scale, norm_shift):
    row_mean = jnp.mean(values, axis=-1, keepdims=True)
    centred = values - row_mean
    spread = jnp.mean(centred * centred, axis=-1, keepdims=True)
    return centred * lax.rsqrt(spread + norm_epsilon) * norm_scale + norm_shift


def dot(a, b):
    return jnp.dot(a, b, preferred_element_type=f32)


def place_of(cores):
    return lax.axis_index("seg") * cores + lax.axis_index("head")


def target(index, cores):
    return {"seg": index // cores, "head": lax.rem(index, cores)}


def greet(me, devs, cores):
    barrier = pltpu.get_barrier_semaphore()
    for label in range(PEERS):
        if label != BACK:
            sender = lax.rem(me - (label - BACK) + devs, devs)
            pl.semaphore_signal(
                barrier, inc=1, device_id=target(sender, cores), device_id_type=MESH
            )
    pl.semaphore_wait(barrier, PEERS - 1)


def halo_kernel(
    devs, cores, feat, picks, ucol, urow, halo, places, slots, outgoing, mine,
    landed, hs, hr, ps, pr,
):
    rows, channels = feat.shape
    width = picks.shape[0]
    me = place_of(cores)
    shift = int(math.log2(rows))
    units = ucol.shape[0]

    def labels(unit_places):
        lab = lax.shift_right_logical(unit_places, jnp.full_like(unit_places, shift)) - me + BACK
        lab = jnp.where(lab < 0, lab + devs, lab)
        return jnp.where(lab >= devs, lab - devs, lab)

    lab_col = labels(ucol[...])
    lab_row = labels(urow[...])
    first = lax.broadcasted_iota(jnp.int32, (units, units), 0)
    second = lax.broadcasted_iota(jnp.int32, (units, units), 1)
    rank = jnp.sum(jnp.where((lab_col == lab_row) & (first < second), 1, 0), axis=0, keepdims=True)
    slot = lab_row * UNITS_PER_PEER + rank
    slots[...] = slot
    slot_ids = lax.broadcasted_iota(jnp.int32, (PEERS * UNITS_PER_PEER, units), 0)
    own = jnp.sum(jnp.where(slot_ids == slot, urow[...] + 1, 0), axis=1, keepdims=True) - 1
    mine[...] = jnp.broadcast_to(own, mine.shape)

    row_ids = lax.broadcasted_iota(jnp.int32, (width, rows), 1)
    for j in range(4):
        table = (picks[:, j : j + 1] == row_ids).astype(f32).astype(bf16)
        outgoing[pl.ds(j * width, width), :] = dot(table, feat[...]).astype(bf16)

    greet(me, devs, cores)

    def halo_copy(j):
        part = pl.ds(j * width, width)
        there = jnp.clip(me + halo_offsets[j], 0, devs - 1)
        return pltpu.make_async_remote_copy(
            src_ref=outgoing.at[part], dst_ref=halo.at[part],
            send_sem=hs.at[j], recv_sem=hr.at[j],
            device_id=target(there, cores), device_id_type=MESH,
        )

    def place_copy(label):
        part = pl.ds(label * UNITS_PER_PEER, UNITS_PER_PEER)
        there = lax.rem(me + (label - BACK) + devs, devs)
        return pltpu.make_async_remote_copy(
            src_ref=mine.at[part], dst_ref=landed.at[part],
            send_sem=ps.at[label], recv_sem=pr.at[label],
            device_id=target(there, cores), device_id_type=MESH,
        )

    def sends(j):
        there = me + halo_offsets[j]
        return (there >= 0) & (there < devs)

    def receives(j):
        source = me - halo_offsets[j]
        return (source >= 0) & (source < devs)

    for j in range(4):
        pl.when(sends(j))(lambda j=j: halo_copy(j).start())
    for label in range(PEERS):
        if label != BACK:
            place_copy(label).start()
    home = pl.ds(BACK * UNITS_PER_PEER, UNITS_PER_PEER)
    landed[home, :] = mine[home, :]
    for j in range(4):
        part = pl.ds(j * width, width)

        @pl.when(jnp.logical_not(receives(j)))
        def _():
            halo[part, :] = jnp.zeros((width, channels), bf16)

    for j in range(4):
        pl.when(sends(j))(lambda j=j: halo_copy(j).wait_send())
        pl.when(receives(j))(lambda j=j: halo_copy(j).wait_recv())
    for label in range(PEERS):
        if label != BACK:
            place_copy(label).wait()
    arrived = landed[...]
    places[...] = jnp.where(arrived >= 0, arrived - me * rows, rows)


def swap_kernel(devs, cores, bucket, arrived, ss, rs, ls):
    me = place_of(cores)
    span = bucket.shape[0] // PEERS

    def copy(label):
        part = pl.ds(label * span, span)
        there = lax.rem(me + (label - BACK) + devs, devs)
        return pltpu.make_async_remote_copy(
            src_ref=bucket.at[part], dst_ref=arrived.at[part],
            send_sem=ss.at[label], recv_sem=rs.at[label],
            device_id=target(there, cores), device_id_type=MESH,
        )

    greet(me, devs, cores)
    others = [label for label in range(PEERS) if label != BACK]
    for label in others:
        copy(label).start()
    part = pl.ds(BACK * span, span)
    local = pltpu.make_async_copy(bucket.at[part], arrived.at[part], ls)
    local.start()
    local.wait()
    for label in others:
        copy(label).wait()


def conv_kernel(
    feat, halo, nbr, slots, conv_w, conv_b, cpe_w, cpe_b, gain, shift, bucket,
    table, acc, lifted,
):
    rows, channels = feat.shape
    taps = nbr.shape[1]
    total = rows + halo.shape[0]
    half = total // 2
    table[:, :channels] = feat[pl.ds(0, half), :]
    table[pl.ds(0, rows - half), channels:] = feat[pl.ds(half, rows - half), :]
    table[pl.ds(rows - half, total - rows), channels:] = halo[...]
    centre = taps // 2
    others = [k for k in range(taps) if k != centre]
    block = 512

    def row_block(b, carry):
        part = pl.ds(pl.multiple_of(b * block, block), block)
        lanes = lax.broadcasted_iota(jnp.int32, (block, half), 1)
        total_sum = dot(feat[part, :], conv_w[centre]) + conv_b[...]
        for n in range(0, len(others), 2):
            pair = []
            for k in others[n : n + 2]:
                ids = nbr[part, k : k + 1]
                upper = ids >= half
                local = jnp.where(upper, ids - half, ids)
                hot = (local == lanes).astype(f32).astype(bf16)
                both = dot(hot, table[...])
                pair.append(jnp.where(upper, both[:, channels:], both[:, :channels]).astype(bf16))
            weight = jnp.concatenate([conv_w[k] for k in others[n : n + 2]], axis=0)
            total_sum = total_sum + dot(jnp.concatenate(pair, axis=1), weight)
        encoded = dot(total_sum.astype(bf16), cpe_w[...]) + cpe_b[...]
        own = feat[part, :].astype(f32)
        lifted[part, :] = (own + normalize(encoded, gain[0:1, :], shift[0:1, :])).astype(bf16)
        return carry

    lax.fori_loop(0, rows // block, row_block, 0)
    bucket[...] = jnp.zeros_like(bucket)
    for u in range(rows // UNIT):
        slot = slots[0, u]
        bucket[pl.ds(pl.multiple_of(slot * UNIT, UNIT), UNIT), :] = lifted[pl.ds(u * UNIT, UNIT), :]


def patch_kernel(
    places, arrived, gain, shift, qkv_w, qkv_b, proj_w, proj_b, fc1_w, fc1_b,
    fc2_w, fc2_b, out, arranged, queries, keys, values,
):
    rows, channels = out.shape
    depth = channels // HEADS

    def put(s, carry):
        row = pl.multiple_of(places[s, 0], UNIT)
        arranged[pl.ds(row, UNIT), :] = arrived[pl.ds(pl.multiple_of(s * UNIT, UNIT), UNIT), :]
        return carry

    lax.fori_loop(0, PEERS * UNITS_PER_PEER, put, 0, unroll=8)
    source = arranged[pl.ds(0, rows), :].astype(f32)
    normed = normalize(source, gain[1:2, :], shift[1:2, :]).astype(bf16)
    joined = (dot(normed, qkv_w[...]) + qkv_b[...]).astype(bf16)
    queries[...] = (joined[:, :channels].astype(f32) * depth ** (-0.5)).astype(bf16)
    turned = jnp.transpose(joined[:, channels : 2 * channels].astype(f32))
    rows_of = lax.broadcasted_iota(jnp.int32, (channels, rows), 0) // depth
    vals = joined[:, 2 * channels :].astype(f32)
    lanes_of = lax.broadcasted_iota(jnp.int32, (rows, channels), 1) // depth
    for h in range(HEADS):
        keys[h] = jnp.where(rows_of == h, turned, 0.0).astype(bf16)
        values[h, :, :channels] = jnp.where(lanes_of == h, vals, 0.0).astype(bf16)
        values[h, :, channels:] = jnp.where(lanes_of == h, 1.0, 0.0).astype(bf16)
    block = 256

    def row_block(b, carry):
        part = pl.ds(pl.multiple_of(b * block, block), block)
        query = queries[part, :]
        sums = jnp.zeros((block, 2 * channels), f32)
        for h in range(HEADS):
            scores = dot(query, keys[h])
            row_max = jnp.max(scores, axis=-1, keepdims=True)
            weights = jnp.exp(scores - row_max).astype(bf16)
            sums = sums + dot(weights, values[h])
        attended = (sums[:, :channels] / sums[:, channels:]).astype(bf16)
        middle = arranged[part, :].astype(f32) + dot(attended, proj_w[...]) + proj_b[...]
        normed_mid = normalize(middle, gain[2:3, :], shift[2:3, :]).astype(bf16)
        raw = dot(normed_mid, fc1_w[...]) + fc1_b[...]
        hidden = (0.5 * raw * (1.0 + lax.erf(raw * (0.5 ** 0.5)))).astype(bf16)
        out[part, :] = (middle + dot(hidden, fc2_w[...]) + fc2_b[...]).astype(bf16)
        return carry

    lax.fori_loop(0, rows // block, row_block, 0)


def per_device(
    features, positions, neighbors, send_rows, conv_weight, conv_bias, cpe_weight,
    cpe_bias, norm_gain, norm_bias, qkv_weight, qkv_bias, proj_weight, proj_bias,
    fc1_weight, fc1_bias, fc2_weight, fc2_bias,
):
    rows, channels = features.shape
    cores = lax.axis_size("head")
    devs = lax.axis_size("seg") * cores
    width = send_rows.shape[1]
    units = rows // UNIT
    slot_count = PEERS * UNITS_PER_PEER
    dma = pltpu.SemaphoreType.DMA
    unit_places = positions.reshape(units, UNIT)[:, 0]
    limit = 48 * 1024 * 1024

    halo, places, slots = pl.pallas_call(
        functools.partial(halo_kernel, devs, cores),
        out_shape=(
            jax.ShapeDtypeStruct((4 * width, channels), bf16),
            jax.ShapeDtypeStruct((slot_count, 128), jnp.int32),
            jax.ShapeDtypeStruct((1, units), jnp.int32),
        ),
        in_specs=[VM] * 4,
        out_specs=(VM, VM, VM),
        scratch_shapes=[
            pltpu.VMEM((4 * width, channels), bf16),
            pltpu.VMEM((slot_count, 128), jnp.int32),
            pltpu.VMEM((slot_count, 128), jnp.int32),
            dma((4,)), dma((4,)), dma((PEERS,)), dma((PEERS,)),
        ],
        compiler_params=pltpu.CompilerParams(
            collective_id=0, has_side_effects=True, vmem_limit_bytes=limit
        ),
        name="halo",
    )(features, send_rows.T, unit_places[:, None], unit_places[None, :])

    bucket = pl.pallas_call(
        conv_kernel,
        out_shape=jax.ShapeDtypeStruct((slot_count * UNIT, channels), bf16),
        in_specs=[VM, VM, VM, SM] + [VM] * 6,
        out_specs=VM,
        scratch_shapes=[
            pltpu.VMEM(((rows + 4 * width) // 2, 2 * channels), bf16),
            pltpu.VMEM((rows, channels), f32),
            pltpu.VMEM((rows, channels), bf16),
        ],
        compiler_params=pltpu.CompilerParams(vmem_limit_bytes=limit),
        name="conv",
    )(
        features, halo, neighbors, slots, conv_weight, conv_bias[None], cpe_weight,
        cpe_bias[None], norm_gain, norm_bias,
    )

    arrived = pl.pallas_call(
        functools.partial(swap_kernel, devs, cores),
        out_shape=jax.ShapeDtypeStruct(bucket.shape, bf16),
        in_specs=[VM],
        out_specs=VM,
        scratch_shapes=[dma((PEERS,)), dma((PEERS,)), dma],
        compiler_params=pltpu.CompilerParams(
            collective_id=1, has_side_effects=True, vmem_limit_bytes=limit
        ),
        name="swap",
    )(bucket)

    return pl.pallas_call(
        patch_kernel,
        out_shape=jax.ShapeDtypeStruct((rows, channels), bf16),
        in_specs=[SM] + [VM] * 11,
        out_specs=VM,
        scratch_shapes=[
            pltpu.VMEM((rows + UNIT, channels), bf16),
            pltpu.VMEM((rows, channels), bf16),
            pltpu.VMEM((HEADS, channels, rows), bf16),
            pltpu.VMEM((HEADS, rows, 2 * channels), bf16),
        ],
        compiler_params=pltpu.CompilerParams(vmem_limit_bytes=limit),
        name="patch",
    )(
        places, arrived, norm_gain, norm_bias, qkv_weight, qkv_bias[None], proj_weight,
        proj_bias[None], fc1_weight, fc1_bias[None], fc2_weight, fc2_bias[None],
    )


def solution(mesh):
    split = P(("groups", "seg", "head"), None)
    placed = (split, P(("groups", "seg", "head")), split, split) + (P(),) * 14
    return jax.shard_map(
        per_device, mesh=mesh, in_specs=placed, out_specs=split, check_vma=False
    )
```

time: 161 us -> 67 us (0.42)
  local copies, waits for them, and re-layouts: 79.7 us -> 4.68 us
  Pallas kernels: 0 us -> 61.9 us
  matrix products: 31.3 us -> 0 us
  starting transfers between devices: 25.4 us -> 0 us
  waiting for transfers between devices: 12.9 us -> 0 us
  other arithmetic: 9.65 us -> 0 us
    pallas_call x0 -> x4, Pallas kernels: none -> 61.9 us  [the longest x1 19.1 us: per_device(): pl.pallas_call(patch_kernel, out_shape=jax.ShapeDtypeStruct((rows, channe...]
    gather x2 -> x0, local copies, waits for them, and re-layouts: 56.7 us -> none  [conv_block(): gathered = row_table[safe_ids]]
    dot_general x27 -> x0, matrix products: 31.3 us -> none  [the longest x8 6.96 us: one_head(): jnp.dot(weights, value_rows, preferred_element_type=jnp.float32)]
    reshape x6 -> x1, local copies, waits for them, and re-layouts: 17.2 us -> 0.07 us  [per_device(): unit_places = positions.reshape(units, UNIT)[:, 0]]
    all_to_all x2 -> x0, starting transfers between devices: 16 us -> none  [the longest x1 10 us: per_device(): lax.all_to_all(bucket_places, ('seg', 'head'), split_axis=0, concat_axis=...]
    all_to_all x2 -> x0, waiting for transfers between devices: 12.9 us -> none  [the longest x1 12.9 us: per_device(): lax.all_to_all(bucket, ('seg', 'head'), split_axis=0, concat_axis=0, tile...]
    ppermute x4 -> x0, starting transfers between devices: 9.39 us -> none  [passed_along(): return lax.ppermute(block, axis, route)]
    reduce_sum x15 -> x0, other arithmetic: 7.34 us -> none  [the longest x8 5.84 us: one_head(): jnp.sum(exp_scores, axis=-1, keepdims=True)]
  transfers between devices with their start and end apart: 6 -> 0, of which waited for: 1 -> 0; matrix products, arithmetic and copies ran while one was open for 57% -> 0% of each run, Pallas kernels for 0% -> 0%
where the time goes in v1:
time: 67 us; the launch traced here: 66.8 us
  Pallas kernels  61.9 us (92%)
  local copies, waits for them, and re-layouts  4.68 us (7%)
    pallas_call x1, Pallas kernels, per_device(): pl.pallas_call(patch_kernel, out_shape=jax.ShapeDtypeStruct((rows, channe...  19.1 us
    pallas_call x1, Pallas kernels, per_device(): pl.pallas_call(functools.partial(swap_kernel, devs, cores), out_shape=jax...  16.5 us
    pallas_call x1, Pallas kernels, per_device(): pl.pallas_call(conv_kernel, out_shape=jax.ShapeDtypeStruct((slot_count *...  15.1 us
    pallas_call x1, Pallas kernels, per_device(): pl.pallas_call(functools.partial(halo_kernel, devs, cores), out_shape=(ja...  11.1 us
    unnamed x38, local copies, waits for them, and re-layouts  4.49 us

profile of v1, /device:TPU:0, one launch (start us, length us, event | category | flops | bytes accessed | tf_op | source)
XLA Modules:
  0.0 66.8 jit_solution(3623977673839583501)
XLA Ops:
  0.0 0.8 %copy.21 = s32[4,128]{0,1:T(8,128)S(1)} copy(s32[4,128]{1,0:T(4,128)} %param.21) | data formatting | bytes 4096 | tf_op args[3]
  0.8 0.0 copy-done.16
  0.8 0.1 reshape.3
  0.9 0.1 slice_reduce_fusion
  1.0 0.0 copy-start
  1.0 0.9 %copy-done = bf16[1024,128]{1,0:T(8,128)(2,1)S(1)} copy-done((bf16[1024,128]{1,0:T(8,128)(2,1)S(1)}, bf16[1024,128]{1,0:T(8,128)(2,1)}, u32[]{:S(2)}) %copy-start) | copy-done | bytes 262168
  2.0 11.1 %halo.1 = (bf16[512,128]{1,0:T(8,128)(2,1)S(1)}, s32[128,128]{1,0:T(8,128)S(1)}, s32[1,64]{1,0:T(1,128)S(1)}) custom-call(bf16[1024,128]{1,0:T(8,128)(2,1)S(1)} %copy-done, s32[128,4]{1,0:T(8,128)S(1)} %bitcast.7, s32[64,1]{1,0:T(8,128)S(1)} %get-tuple-element.12.ucol, s32[1,64]{1,0:T(1,128)S(1)} %bitcast.9), custom_call_target="tpu_custom_call" | custom-call | tf_op jit(solution)/shard_map/halo/pallas_call | solution.py:268
  13.1 0.0 copy-start.1
  13.1 0.0 copy-start.6
  13.1 0.2 copy.22.nbr
  13.3 0.0 copy-start.9
  13.4 0.0 copy-start.8
  13.4 0.0 copy-start.11
  13.4 0.0 copy-start.12
  13.4 0.7 copy-done.1
  14.1 0.0 copy-done.8
  14.1 0.0 copy-start.2
  14.1 1.2 %copy-done.2 = bf16[27,128,128]{2,1,0:T(8,128)(2,1)S(1)} copy-done((bf16[27,128,128]{2,1,0:T(8,128)(2,1)S(1)}, bf16[27,128,128]{2,1,0:T(8,128)(2,1)}, u32[]{:S(2)}) %copy-start.2) | copy-done | bytes 884760
  15.2 15.1 %conv.1.bucket = bf16[2048,128]{1,0:T(8,128)(2,1)S(1)} custom-call(bf16[1024,128]{1,0:T(8,128)(2,1)S(1)} %copy-done.1, bf16[512,128]{1,0:T(8,128)(2,1)S(1)} %get-tuple-element.9.halo, s32[1024,27]{1,0:T(8,128)S(1)} %copy.22.nbr, s32[1,64]{1,0:T(1,128)S(1)} %get-tuple-element.10.slots, bf16[27,128,128]{2,1,0:T(8,128)(2,1)S(1)} %copy-done.2, ...), custom_call_target="tpu_custom_call" | custom-call | tf_op jit(solution)/shard_map/conv/pallas_call | solution.py:289
  30.3 0.0 copy-start.17
  30.4 0.0 copy-start.3
  30.4 0.0 copy-start.4
  30.4 0.0 copy-start.5
  30.4 0.0 copy-start.7
  30.4 16.5 %swap.1.arrived = bf16[2048,128]{1,0:T(8,128)(2,1)S(1)} custom-call(bf16[2048,128]{1,0:T(8,128)(2,1)S(1)} %conv.1.bucket), custom_call_target="tpu_custom_call" | custom-call | tf_op jit(solution)/shard_map/swap/pallas_call | solution.py:306
  46.9 0.0 copy-done.17
  46.9 0.0 copy-start.10
  47.0 0.0 copy-start.13
  47.0 0.0 copy-start.14
  47.0 0.6 copy-done.10
  47.6 0.0 copy-done.13
  47.6 19.1 %patch.1 = bf16[1024,128]{1,0:T(8,128)(2,1)} custom-call(s32[128,128]{1,0:T(8,128)S(1)} %get-tuple-element.8.places, bf16[2048,128]{1,0:T(8,128)(2,1)S(1)} %swap.1.arrived, f32[3,128]{1,0:T(4,128)S(1)} %copy-done.8, f32[3,128]{1,0:T(4,128)S(1)} %copy-done.9, bf16[128,384]{1,0:T(8,128)(2,1)S(1)} %copy-done.5, f32[1,384]{1,0:T(1,128)S(1)} %broadcast_in_dim.20.qkv_b, ...), custom_call_target="tpu_custom_call" | custom-call | tf_op jit(solution)/shard_map/patch/pallas_call | solution.py:318
  (13 shorter events, 0.0 us)
Async XLA Ops:
  0.0 0.8 %copy-start.16 = (s32[1024]{0:T(1024)S(1)}, s32[1024]{0:T(1024)}, u32[]{:S(2)}) copy-start(s32[1024]{0:T(1024)} %param.19) | copy-start | bytes 12292
  1.0 1.0 %copy-start = (bf16[1024,128]{1,0:T(8,128)(2,1)S(1)}, bf16[1024,128]{1,0:T(8,128)(2,1)}, u32[]{:S(2)}) copy-start(bf16[1024,128]{1,0:T(8,128)(2,1)} %feat.3) | copy-start | bytes 786436
  2.0 11.1 %copy-start.15 = (s32[1024,27]{0,1:T(8,128)S(1)}, s32[1024,27]{0,1:T(8,128)}, u32[]{:S(2)}) copy-start(s32[1024,27]{0,1:T(8,128)} %param.20) | copy-start | bytes 331780
  13.1 1.0 %copy-start.1 = (bf16[1024,128]{1,0:T(8,128)(2,1)S(1)}, bf16[1024,128]{1,0:T(8,128)(2,1)}, u32[]{:S(2)}) copy-start(bf16[1024,128]{1,0:T(8,128)(2,1)} %feat.3) | copy-start | bytes 786436
  13.1 0.9 %copy-start.6 = (bf16[128,128]{1,0:T(8,128)(2,1)S(1)}, bf16[128,128]{1,0:T(8,128)(2,1)}, u32[]{:S(2)}) copy-start(bf16[128,128]{1,0:T(8,128)(2,1)} %cpe_w.1) | copy-start | bytes 98308
  13.3 0.7 %copy-start.9 = (f32[3,128]{1,0:T(4,128)S(1)}, f32[3,128]{1,0:T(4,128)}, u32[]{:S(2)}) copy-start(f32[3,128]{1,0:T(4,128)} %shift.3) | copy-start | bytes 4612
  13.4 0.7 %copy-start.8 = (f32[3,128]{1,0:T(4,128)S(1)}, f32[3,128]{1,0:T(4,128)}, u32[]{:S(2)}) copy-start(f32[3,128]{1,0:T(4,128)} %gain.3) | copy-start | bytes 4612
  13.4 0.7 %copy-start.11 = (f32[128]{0:T(128)S(1)}, f32[128]{0:T(128)}, u32[]{:S(2)}) copy-start(f32[128]{0:T(128)} %param.23) | copy-start | bytes 1540
  13.4 0.7 %copy-start.12 = (f32[128]{0:T(128)S(1)}, f32[128]{0:T(128)}, u32[]{:S(2)}) copy-start(f32[128]{0:T(128)} %param.25) | copy-start | bytes 1540
  14.1 1.2 %copy-start.2 = (bf16[27,128,128]{2,1,0:T(8,128)(2,1)S(1)}, bf16[27,128,128]{2,1,0:T(8,128)(2,1)}, u32[]{:S(2)}) copy-start(bf16[27,128,128]{2,1,0:T(8,128)(2,1)} %conv_w.1) | copy-start | bytes 2654212
  30.3 16.6 %copy-start.17 = (f32[384]{0:T(512)S(1)}, f32[384]{0:T(512)}, u32[]{:S(2)}) copy-start(f32[384]{0:T(512)} %param.29) | copy-start | bytes 4612
  30.4 16.6 %copy-start.3 = (bf16[128,512]{1,0:T(8,128)(2,1)S(1)}, bf16[128,512]{1,0:T(8,128)(2,1)}, u32[]{:S(2)}) copy-start(bf16[128,512]{1,0:T(8,128)(2,1)} %fc1_w.1) | copy-start | bytes 393220
  30.4 16.6 %copy-start.4 = (bf16[512,128]{1,0:T(8,128)(2,1)S(1)}, bf16[512,128]{1,0:T(8,128)(2,1)}, u32[]{:S(2)}) copy-start(bf16[512,128]{1,0:T(8,128)(2,1)} %fc2_w.1) | copy-start | bytes 393220
  30.4 16.6 %copy-start.5 = (bf16[128,384]{1,0:T(8,128)(2,1)S(1)}, bf16[128,384]{1,0:T(8,128)(2,1)}, u32[]{:S(2)}) copy-start(bf16[128,384]{1,0:T(8,128)(2,1)} %qkv_w.1) | copy-start | bytes 294916
  30.4 16.6 %copy-start.7 = (bf16[128,128]{1,0:T(8,128)(2,1)S(1)}, bf16[128,128]{1,0:T(8,128)(2,1)}, u32[]{:S(2)}) copy-start(bf16[128,128]{1,0:T(8,128)(2,1)} %proj_w.1) | copy-start | bytes 98308
  46.9 0.7 %copy-start.10 = (f32[512]{0:T(512)S(1)}, f32[512]{0:T(512)}, u32[]{:S(2)}) copy-start(f32[512]{0:T(512)} %param.33) | copy-start | bytes 6148
  47.0 0.7 %copy-start.13 = (f32[128]{0:T(128)S(1)}, f32[128]{0:T(128)}, u32[]{:S(2)}) copy-start(f32[128]{0:T(128)} %param.31) | copy-start | bytes 1540
  47.0 0.7 copy-start.14

commit v2 on v1

v2 whole, which is shorter than its diff:
```python
import functools
import math

import jax
import jax.numpy as jnp
from jax import lax
from jax.experimental import pallas as pl
from jax.experimental.pallas import tpu as pltpu
from jax.sharding import PartitionSpec as P

HEADS = 8
PEERS = 16
BACK = 7
UNITS_PER_PEER = 8
UNIT = 16

norm_epsilon = 1e-05
halo_offsets = (1, 2, -1, -2)
MESH = pl.DeviceIdType.MESH
VM = pl.BlockSpec(memory_space=pltpu.VMEM)
SM = pl.BlockSpec(memory_space=pltpu.SMEM)
f32 = jnp.float32
bf16 = jnp.bfloat16


def normalize(values, norm_scale, norm_shift):
    row_mean = jnp.mean(values, axis=-1, keepdims=True)
    centred = values - row_mean
    spread = jnp.mean(centred * centred, axis=-1, keepdims=True)
    return centred * lax.rsqrt(spread + norm_epsilon) * norm_scale + norm_shift


def dot(a, b):
    return jnp.dot(a, b, preferred_element_type=f32)


def place_of(cores):
    return lax.axis_index("seg") * cores + lax.axis_index("head")


def target(index, cores):
    return {"seg": index // cores, "head": lax.rem(index, cores)}


def ahead(me, step, devs):
    if devs == PEERS:
        half = devs // 2
        mine = me // half
        across = (1 - mine) * half + lax.rem(me + step, half)
        beside = mine * half + lax.rem(me + step + 1, half)
        return jnp.where(step < half, across, beside)
    return lax.rem(me + jnp.where(step < PEERS // 2, PEERS // 2 - step, PEERS // 2 - 1 - step + devs)
                   + jnp.where(step == PEERS - 1, PEERS // 2 , 0), devs)


def step_of(dest, me, devs):
    if devs == PEERS:
        half = devs // 2
        far = (dest >= half) != (me >= half)
        gap = dest - me
        return jnp.where(far, (gap + devs) & (half - 1), half + ((gap - 1 + devs) & (half - 1)))
    gap = dest - me
    gap = jnp.where(gap < -BACK, gap + devs, gap)
    gap = jnp.where(gap > PEERS // 2, gap - devs, gap)
    return jnp.where(gap > 0, PEERS // 2 - gap, jnp.where(gap == 0, PEERS - 1, PEERS // 2 - 1 - gap))


def label_of(dest, me, devs):
    return lax.rem(dest - me + BACK + devs, devs)


def conv_kernel(
    devs, cores, feat, picks, ucol, urow, prow, nbr, conv_w, conv_b, cpe_w, cpe_b, gain, shift,
    arrived, places, halo, outgoing, mine, landed, bucket, table, wide, cols, uppers, own,
    acc, lifted, hs, hr, ps, pr, ss, rs,
):
    rows, channels = feat.shape
    width = picks.shape[0]
    units = ucol.shape[0]
    taps = nbr.shape[1]
    me = place_of(cores)
    log_rows = int(math.log2(rows))
    log_unit = int(math.log2(UNIT))
    span = UNITS_PER_PEER * UNIT
    half = rows // 2

    barrier = pltpu.get_barrier_semaphore()
    for label in range(PEERS):
        if label != BACK:
            sender = lax.rem(me - (label - BACK) + devs, devs)
            pl.semaphore_signal(
                barrier, inc=1, device_id=target(sender, cores), device_id_type=MESH
            )

    def steps(unit_places):
        return step_of(lax.shift_right_logical(unit_places, jnp.full_like(unit_places, log_rows)), me, devs)

    step_col = steps(ucol[...])
    step_row = steps(urow[...])
    first = lax.broadcasted_iota(jnp.int32, (units, units), 0)
    second = lax.broadcasted_iota(jnp.int32, (units, units), 1)
    rank = jnp.sum(jnp.where((step_col == step_row) & (first < second), 1, 0), axis=0, keepdims=True)
    slot = step_row * UNITS_PER_PEER + rank
    slot_ids = lax.broadcasted_iota(jnp.int32, (PEERS * UNITS_PER_PEER, units), 0)
    sent = jnp.sum(jnp.where(slot_ids == slot, urow[...] + 1, 0), axis=1, keepdims=True) - 1
    mine[...] = jnp.broadcast_to(sent, mine.shape)

    row_ids = lax.broadcasted_iota(jnp.int32, (width, rows), 1)
    for j in range(4):
        hot = (picks[:, j : j + 1] == row_ids).astype(f32).astype(bf16)
        outgoing[pl.ds(j * width, width), :] = dot(hot, feat[...]).astype(bf16)

    def halo_copy(j):
        part = pl.ds(j * width, width)
        there = jnp.clip(me + halo_offsets[j], 0, devs - 1)
        return pltpu.make_async_remote_copy(
            src_ref=outgoing.at[part], dst_ref=halo.at[part],
            send_sem=hs.at[j], recv_sem=hr.at[j],
            device_id=target(there, cores), device_id_type=MESH,
        )

    def sends(j):
        there = me + halo_offsets[j]
        return (there >= 0) & (there < devs)

    def receives(j):
        source = me - halo_offsets[j]
        return (source >= 0) & (source < devs)

    def place_copy(step, label=None):
        there = ahead(me, step, devs)
        label = label_of(there, me, devs) if label is None else label
        return pltpu.make_async_remote_copy(
            src_ref=mine.at[pl.ds(pl.multiple_of(step * UNITS_PER_PEER, UNITS_PER_PEER), UNITS_PER_PEER)],
            dst_ref=landed.at[pl.ds(pl.multiple_of(label * UNITS_PER_PEER, UNITS_PER_PEER), UNITS_PER_PEER)],
            send_sem=ps.at[step], recv_sem=pr.at[label],
            device_id=target(there, cores), device_id_type=MESH,
        )

    def row_copy(step, label=None):
        there = ahead(me, step, devs)
        label = label_of(there, me, devs) if label is None else label
        return pltpu.make_async_remote_copy(
            src_ref=bucket.at[pl.ds(pl.multiple_of(step * span, span), span)],
            dst_ref=arrived.at[pl.ds(pl.multiple_of(label * span, span), span)],
            send_sem=ss.at[step], recv_sem=rs.at[label],
            device_id=target(there, cores), device_id_type=MESH,
        )

    pl.semaphore_wait(barrier, PEERS - 1)
    for j in range(4):
        pl.when(sends(j))(lambda j=j: halo_copy(j).start())
    for step in range(PEERS - 1):
        place_copy(jnp.int32(step)).start()

    table[pl.ds(0, half), :channels] = feat[pl.ds(0, half), :]
    table[pl.ds(0, half), channels:] = feat[pl.ds(half, half), :]
    lifted[...] = jnp.zeros_like(lifted)

    row_steps = steps(prow[...])
    unit_of = lax.shift_right_logical(
        lax.broadcasted_iota(jnp.int32, (1, rows), 1), jnp.full((1, rows), log_unit, jnp.int32)
    )
    unit_col = lax.broadcasted_iota(jnp.int32, (units, 1), 0)
    before = (step_col < row_steps) | ((step_col == row_steps) & (unit_col < unit_of))
    rank_row = jnp.sum(jnp.where(before, 1, 0), axis=0, keepdims=True)
    dest_row = rank_row * UNIT + (lax.broadcasted_iota(jnp.int32, (1, rows), 1) & (UNIT - 1))
    codes = nbr[...] + 1
    high = lax.shift_right_logical(codes, jnp.full_like(codes, 5))
    wide[:, :channels] = feat[...]
    wide[:, channels:] = jnp.zeros((rows, channels), bf16)
    wide[:, channels : channels + taps] = high.astype(f32).astype(bf16)
    wide[:, channels + 32 : channels + 32 + taps] = (codes & 31).astype(f32).astype(bf16)
    sort = (lax.broadcasted_iota(jnp.int32, (rows, rows), 0) == dest_row).astype(f32).astype(bf16)
    ordered = dot(sort, wide[...])
    own[...] = ordered[:, :channels].astype(bf16)
    ids = (
        ordered[:, channels : channels + 32] * 32.0 + ordered[:, channels + 32 : channels + 64] - 1.0
    ).astype(jnp.int32)
    away = ids >= rows
    upper = (ids >= rows + 2 * width) | ((ids >= half) & (ids < rows))
    cols[...] = jnp.where(
        away,
        half + ids - rows - jnp.where(upper, 2 * width, 0),
        ids - jnp.where(upper, half, 0),
    )
    uppers[...] = jnp.where(upper, 1, 0)

    centre = taps // 2
    others = [k for k in range(taps) if k != centre]
    block = 256
    group = 2

    def conv_pass(b, base, depth, start):
        part = pl.ds(pl.multiple_of(b * block, block), block)
        lanes = lax.broadcasted_iota(jnp.int32, (block, depth), 1) + base
        total = start
        for n in range(0, len(others), group):
            ks = others[n : n + group]
            hot = jnp.concatenate(
                [(cols[part, k : k + 1] == lanes).astype(f32).astype(bf16) for k in ks], axis=0
            )
            both = dot(hot, table[pl.ds(base, depth), :])
            chosen = []
            for i, k in enumerate(ks):
                piece = both[i * block : (i + 1) * block]
                chosen.append(
                    jnp.where(uppers[part, k : k + 1] > 0, piece[:, channels:], piece[:, :channels]).astype(bf16)
                )
            weight = jnp.concatenate([conv_w[k] for k in ks], axis=0)
            total = total + dot(jnp.concatenate(chosen, axis=1), weight)
        return total

    def begun(b):
        part = pl.ds(pl.multiple_of(b * block, block), block)
        return dot(own[part, :], conv_w[centre]) + conv_b[...]

    def local_block(b, carry):
        acc[pl.ds(pl.multiple_of(b * block, block), block), :] = conv_pass(b, 0, half, begun(b))
        return carry

    def pack(start, count):
        slot_rows = count * span
        q = lax.broadcasted_iota(jnp.int32, (slot_rows, 1), 0) + start * span
        step = lax.shift_right_logical(q, jnp.full_like(q, int(math.log2(span))))
        smaller = jnp.sum(jnp.where(step_row < step, 1, 0), axis=1, keepdims=True)
        source = smaller * UNIT + (q & (span - 1))
        hot = (source == lax.broadcasted_iota(jnp.int32, (slot_rows, rows), 1)).astype(f32).astype(bf16)
        return dot(hot, lifted[...]).astype(bf16)

    def finish(b, total):
        part = pl.ds(pl.multiple_of(b * block, block), block)
        encoded = dot(total.astype(bf16), cpe_w[...]) + cpe_b[...]
        lifted[part, :] = (
            own[part, :].astype(f32) + normalize(encoded, gain[0:1, :], shift[0:1, :])
        ).astype(bf16)
        per = block // span
        bucket[pl.ds(pl.multiple_of(b * block, block), block), :] = pack(b * per, per)
        for i in range(per):
            row_copy(b * per + i).start()

    def halo_block(b, carry):
        part = pl.ds(pl.multiple_of(b * block, block), block)
        finish(b, conv_pass(b, half, 2 * width, acc[part, :]))
        return carry

    def full_block(b, carry):
        finish(b, conv_pass(b, 0, half + 2 * width, begun(b)))
        return carry

    lax.fori_loop(0, 2, local_block, 0)
    for j in range(4):
        pl.when(sends(j))(lambda j=j: halo_copy(j).wait_send())
        pl.when(receives(j))(lambda j=j: halo_copy(j).wait_recv())
        landing = pl.ds(half + (j % 2) * width, width)
        lane_part = pl.ds((j // 2) * channels, channels)

        @pl.when(receives(j))
        def _():
            table[landing, lane_part] = halo[pl.ds(j * width, width), :]

        @pl.when(jnp.logical_not(receives(j)))
        def _():
            table[landing, lane_part] = jnp.zeros((width, channels), bf16)

    lax.fori_loop(0, 2, halo_block, 0)
    lax.fori_loop(2, rows // block, full_block, 0)
    done = rows // span
    rest = pack(done, PEERS - done)
    bucket[pl.ds(rows, (PEERS - done) * span), :] = rest
    for step in range(done, PEERS - 1):
        row_copy(jnp.int32(step)).start()
    arrived[pl.ds(BACK * span, span), :] = bucket[pl.ds((PEERS - 1) * span, span), :]
    home = pl.ds(BACK * UNITS_PER_PEER, UNITS_PER_PEER)
    landed[home, :] = mine[pl.ds((PEERS - 1) * UNITS_PER_PEER, UNITS_PER_PEER), :]
    for step in range(PEERS - 1):
        place_copy(jnp.int32(step)).wait_send()
        row_copy(jnp.int32(step)).wait_send()
    for label in range(PEERS):
        if label != BACK:
            place_copy(jnp.int32(0), label).wait_recv()
            row_copy(jnp.int32(0), label).wait_recv()
    seen = landed[...]
    places[...] = jnp.where(seen >= 0, seen - me * rows, rows)


def patch_kernel(
    places, arrived, gain, shift, qkv_w, qkv_b, proj_w, proj_b, fc1_w, fc1_b,
    fc2_w, fc2_b, out, arranged, queries, keys, values,
):
    rows, channels = out.shape
    depth = channels // HEADS

    def put(s, carry):
        row = pl.multiple_of(places[s, 0], UNIT)
        arranged[pl.ds(row, UNIT), :] = arrived[pl.ds(pl.multiple_of(s * UNIT, UNIT), UNIT), :]
        return carry

    lax.fori_loop(0, PEERS * UNITS_PER_PEER, put, 0, unroll=8)
    source = arranged[pl.ds(0, rows), :].astype(f32)
    normed = normalize(source, gain[1:2, :], shift[1:2, :]).astype(bf16)
    joined = (dot(normed, qkv_w[...]) + qkv_b[...]).astype(bf16)
    queries[...] = (joined[:, :channels].astype(f32) * depth ** (-0.5)).astype(bf16)
    turned = jnp.transpose(joined[:, channels : 2 * channels].astype(f32))
    rows_of = lax.broadcasted_iota(jnp.int32, (channels, rows), 0) // depth
    vals = joined[:, 2 * channels :].astype(f32)
    lanes_of = lax.broadcasted_iota(jnp.int32, (rows, channels), 1) // depth
    for h in range(HEADS):
        keys[h] = jnp.where(rows_of == h, turned, 0.0).astype(bf16)
        values[h, :, :channels] = jnp.where(lanes_of == h, vals, 0.0).astype(bf16)
        values[h, :, channels:] = jnp.where(lanes_of == h, 1.0, 0.0).astype(bf16)
    block = 1024

    def row_block(b, carry):
        part = pl.ds(pl.multiple_of(b * block, block), block)
        query = queries[part, :]
        sums = jnp.zeros((block, 2 * channels), f32)
        for h in range(HEADS):
            scores = dot(query, keys[h])
            row_max = jnp.max(scores, axis=-1, keepdims=True)
            weights = jnp.exp(scores - row_max).astype(bf16)
            sums = sums + dot(weights, values[h])
        attended = (sums[:, :channels] / sums[:, channels:]).astype(bf16)
        middle = arranged[part, :].astype(f32) + dot(attended, proj_w[...]) + proj_b[...]
        normed_mid = normalize(middle, gain[2:3, :], shift[2:3, :]).astype(bf16)
        raw = dot(normed_mid, fc1_w[...]) + fc1_b[...]
        hidden = (0.5 * raw * (1.0 + lax.erf(raw * (0.5 ** 0.5)))).astype(bf16)
        out[part, :] = (middle + dot(hidden, fc2_w[...]) + fc2_b[...]).astype(bf16)
        return carry

    lax.fori_loop(0, rows // block, row_block, 0)


def per_device(
    features, positions, neighbors, send_rows, conv_weight, conv_bias, cpe_weight,
    cpe_bias, norm_gain, norm_bias, qkv_weight, qkv_bias, proj_weight, proj_bias,
    fc1_weight, fc1_bias, fc2_weight, fc2_bias,
):
    rows, channels = features.shape
    cores = lax.axis_size("head")
    devs = lax.axis_size("seg") * cores
    width = send_rows.shape[1]
    units = rows // UNIT
    slot_count = PEERS * UNITS_PER_PEER
    dma = pltpu.SemaphoreType.DMA
    unit_places = positions.reshape(units, UNIT)[:, 0]
    limit = 48 * 1024 * 1024

    i32 = jnp.int32
    arrived, places = pl.pallas_call(
        functools.partial(conv_kernel, devs, cores),
        out_shape=(
            jax.ShapeDtypeStruct((slot_count * UNIT, channels), bf16),
            jax.ShapeDtypeStruct((slot_count, 128), i32),
        ),
        in_specs=[VM] * 12,
        out_specs=(VM, VM),
        scratch_shapes=[
            pltpu.VMEM((4 * width, channels), bf16),
            pltpu.VMEM((4 * width, channels), bf16),
            pltpu.VMEM((slot_count, 128), i32),
            pltpu.VMEM((slot_count, 128), i32),
            pltpu.VMEM((slot_count * UNIT, channels), bf16),
            pltpu.VMEM(((rows + 4 * width) // 2, 2 * channels), bf16),
            pltpu.VMEM((rows, 2 * channels), bf16),
            pltpu.VMEM((rows, 32), i32),
            pltpu.VMEM((rows, 32), i32),
            pltpu.VMEM((rows, channels), bf16),
            pltpu.VMEM((rows, channels), f32),
            pltpu.VMEM((rows, channels), bf16),
            dma((4,)), dma((4,)), dma((PEERS,)), dma((PEERS,)), dma((PEERS,)), dma((PEERS,)),
        ],
        compiler_params=pltpu.CompilerParams(
            collective_id=0, has_side_effects=True, vmem_limit_bytes=limit
        ),
        name="conv",
    )(
        features, send_rows.T, unit_places[:, None], unit_places[None, :], positions[None, :],
        neighbors, conv_weight, conv_bias[None], cpe_weight, cpe_bias[None], norm_gain, norm_bias,
    )

    return pl.pallas_call(
        patch_kernel,
        out_shape=jax.ShapeDtypeStruct((rows, channels), bf16),
        in_specs=[SM] + [VM] * 11,
        out_specs=VM,
        scratch_shapes=[
            pltpu.VMEM((rows + UNIT, channels), bf16),
            pltpu.VMEM((rows, channels), bf16),
            pltpu.VMEM((HEADS, channels, rows), bf16),
            pltpu.VMEM((HEADS, rows, 2 * channels), bf16),
        ],
        compiler_params=pltpu.CompilerParams(vmem_limit_bytes=limit),
        name="patch",
    )(
        places, arrived, norm_gain, norm_bias, qkv_weight, qkv_bias[None], proj_weight,
        proj_bias[None], fc1_weight, fc1_bias[None], fc2_weight, fc2_bias[None],
    )


def solution(mesh):
    split = P(("groups", "seg", "head"), None)
    placed = (split, P(("groups", "seg", "head")), split, split) + (P(),) * 14
    return jax.shard_map(
        per_device, mesh=mesh, in_specs=placed, out_specs=split, check_vma=False
    )
```

time: 67 us -> 70.1 us (1.046)
  Pallas kernels: 61.9 us -> 64.3 us
    pallas_call x3 -> x1, Pallas kernels: 42.7 us -> 47.9 us  [per_device(): pl.pallas_call(functools.partial(conv_kernel, devs, cores), out_shape=(ja...]
    pallas_call x1, Pallas kernels: 19.1 us -> 16.4 us  [per_device(): pl.pallas_call(patch_kernel, out_shape=jax.ShapeDtypeStruct((rows, channe...]
    unnamed x38 -> x36, local copies, waits for them, and re-layouts: 4.49 us -> 4.47 us
where the time goes in v2:
time: 70.1 us; the launch traced here: 69.8 us
  Pallas kernels  64.3 us (92%)
  local copies, waits for them, and re-layouts  5.34 us (8%)
    pallas_call x1, Pallas kernels, per_device(): pl.pallas_call(functools.partial(conv_kernel, devs, cores), out_shape=(ja...  47.9 us
    pallas_call x1, Pallas kernels, per_device(): pl.pallas_call(patch_kernel, out_shape=jax.ShapeDtypeStruct((rows, channe...  16.4 us
    unnamed x36, local copies, waits for them, and re-layouts  4.47 us

profile of v2, /device:TPU:0, one launch (start us, length us, event | category | flops | bytes accessed | tf_op | source)
XLA Modules:
  0.0 69.8 jit_solution(11947641852514539604)
XLA Ops:
  0.0 0.8 %reshape.3 = s32[64,16]{1,0:T(8,128)S(1)} reshape(s32[1024]{0:T(1024)} %param.19) | data formatting | bytes 8192 | tf_op jit(solution)/shard_map/reshape | solution.py:346
  0.8 0.1 slice_reduce_fusion
  0.9 0.0 copy-start.15
  0.9 0.0 copy-start.1
  0.9 1.2 %copy.22.nbr = s32[1024,27]{1,0:T(8,128)S(1)} copy(s32[1024,27]{0,1:T(8,128)} %param.20) | data formatting | bytes 221184 | tf_op args[2]
  2.1 0.0 copy-done.15
  2.1 0.0 copy-start.6
  2.1 0.0 copy-start.9
  2.1 0.1 copy.21
  2.2 0.0 copy-start.7
  2.2 0.0 copy-start.8
  2.2 0.0 copy-start.13
  2.2 0.0 copy-start.14
  2.3 0.0 copy-done.1
  2.3 0.6 copy-done.6
  2.8 0.0 copy-done.9
  2.8 0.1 copy-done.7
  2.9 0.0 copy-done.8
  2.9 0.0 copy-done.13
  2.9 0.0 copy-done.14
  2.9 1.2 %copy-done = bf16[27,128,128]{2,1,0:T(8,128)(2,1)S(1)} copy-done((bf16[27,128,128]{2,1,0:T(8,128)(2,1)S(1)}, bf16[27,128,128]{2,1,0:T(8,128)(2,1)}, u32[]{:S(2)}) %copy-start) | copy-done | bytes 884760
  4.1 47.9 %conv.1 = (bf16[2048,128]{1,0:T(8,128)(2,1)S(1)}, s32[128,128]{1,0:T(8,128)S(1)}) custom-call(bf16[1024,128]{1,0:T(8,128)(2,1)S(1)} %copy-done.1, s32[128,4]{1,0:T(8,128)S(1)} %bitcast.8, s32[64,1]{1,0:T(8,128)S(1)} %get-tuple-element.10.ucol, s32[1,64]{1,0:T(1,128)S(1)} %bitcast.11, s32[1,1024]{1,0:T(1,128)S(1)} %bitcast.9, s32[1024,27]{1,0:T(8,128)S(1)} %copy.22.nbr, ...), custom_call_target="tpu_custom_call" | custom-call | tf_op jit(solution)/shard_map/conv/pallas_call | solution.py:350
  52.1 0.0 copy-start.16
  52.1 0.7 copy-done.16
  52.8 0.0 copy-done.2
  52.8 0.0 copy-done.3
  52.8 0.0 copy-done.4
  52.8 0.0 copy-done.5
  52.8 0.6 copy-done.10
  53.4 0.0 copy-done.11
  53.4 0.0 copy-done.12
  53.4 16.4 %patch.1 = bf16[1024,128]{1,0:T(8,128)(2,1)} custom-call(s32[128,128]{1,0:T(8,128)S(1)} %get-tuple-element.7.places, bf16[2048,128]{1,0:T(8,128)(2,1)S(1)} %get-tuple-element.8.arrived, f32[3,128]{1,0:T(4,128)S(1)} %copy-done.8, f32[3,128]{1,0:T(4,128)S(1)} %copy-done.9, bf16[128,384]{1,0:T(8,128)(2,1)S(1)} %copy-done.4, ...), custom_call_target="tpu_custom_call" | custom-call | tf_op jit(solution)/shard_map/patch/pallas_call | solution.py:382
  (9 shorter events, 0.0 us)
Async XLA Ops:
  0.9 1.2 %copy-start.15 = (s32[4,128]{1,0:T(4,128)S(1)}, s32[4,128]{1,0:T(4,128)}, u32[]{:S(2)}) copy-start(s32[4,128]{1,0:T(4,128)} %param.21) | copy-start | bytes 6148
  0.9 1.4 %copy-start.1 = (bf16[1024,128]{1,0:T(8,128)(2,1)S(1)}, bf16[1024,128]{1,0:T(8,128)(2,1)}, u32[]{:S(2)}) copy-start(bf16[1024,128]{1,0:T(8,128)(2,1)} %feat.1) | copy-start | bytes 786436
  2.1 0.8 %copy-start.6 = (bf16[128,128]{1,0:T(8,128)(2,1)S(1)}, bf16[128,128]{1,0:T(8,128)(2,1)}, u32[]{:S(2)}) copy-start(bf16[128,128]{1,0:T(8,128)(2,1)} %cpe_w.1) | copy-start | bytes 98308
  2.1 0.8 %copy-start.9 = (f32[3,128]{1,0:T(4,128)S(1)}, f32[3,128]{1,0:T(4,128)}, u32[]{:S(2)}) copy-start(f32[3,128]{1,0:T(4,128)} %shift.3) | copy-start | bytes 4612
  2.2 0.7 copy-start.7
  2.2 0.7 copy-start.8
  2.2 0.7 copy-start.13
  2.2 0.7 copy-start.14
  2.9 1.2 %copy-start = (bf16[27,128,128]{2,1,0:T(8,128)(2,1)S(1)}, bf16[27,128,128]{2,1,0:T(8,128)(2,1)}, u32[]{:S(2)}) copy-start(bf16[27,128,128]{2,1,0:T(8,128)(2,1)} %conv_w.1) | copy-start | bytes 2654212
  4.1 48.7 %copy-start.2 = (bf16[128,512]{1,0:T(8,128)(2,1)S(1)}, bf16[128,512]{1,0:T(8,128)(2,1)}, u32[]{:S(2)}) copy-start(bf16[128,512]{1,0:T(8,128)(2,1)} %fc1_w.1) | copy-start | bytes 393220
  4.1 48.7 %copy-start.3 = (bf16[512,128]{1,0:T(8,128)(2,1)S(1)}, bf16[512,128]{1,0:T(8,128)(2,1)}, u32[]{:S(2)}) copy-start(bf16[512,128]{1,0:T(8,128)(2,1)} %fc2_w.1) | copy-start | bytes 393220
  4.1 48.7 %copy-start.4 = (bf16[128,384]{1,0:T(8,128)(2,1)S(1)}, bf16[128,384]{1,0:T(8,128)(2,1)}, u32[]{:S(2)}) copy-start(bf16[128,384]{1,0:T(8,128)(2,1)} %qkv_w.1) | copy-start | bytes 294916
  4.1 48.7 %copy-start.5 = (bf16[128,128]{1,0:T(8,128)(2,1)S(1)}, bf16[128,128]{1,0:T(8,128)(2,1)}, u32[]{:S(2)}) copy-start(bf16[128,128]{1,0:T(8,128)(2,1)} %proj_w.1) | copy-start | bytes 98308
  52.1 0.7 copy-start.16
  52.7 0.7 copy-start.10
  52.8 0.7 copy-start.11
  52.8 0.7 copy-start.12

commit v3 on v1

--- a/solution.py
+++ b/solution.py
@@ -136,12 +136,27 @@
     places[...] = jnp.where(arrived >= 0, arrived - me * rows, rows)
 
 
+def ahead(me, step, devs):
+    if devs == PEERS:
+        half = devs // 2
+        mine = me // half
+        across = (1 - mine) * half + lax.rem(me + step, half)
+        beside = mine * half + lax.rem(me + step + 1, half)
+        return jnp.where(step < half, across, beside)
+    return lax.rem(me + jnp.where(step < PEERS // 2, PEERS // 2 - step, PEERS // 2 - 1 - step + devs)
+                   + jnp.where(step == PEERS - 1, PEERS // 2 , 0), devs)
+
+
+def label_of(dest, me, devs):
+    return lax.rem(dest - me + BACK + devs, devs)
+
+
 def swap_kernel(devs, cores, bucket, arrived, ss, rs, ls):
     me = place_of(cores)
     span = bucket.shape[0] // PEERS
 
     def copy(label):
-        part = pl.ds(label * span, span)
+        part = pl.ds(pl.multiple_of(label * span, span), span)
         there = lax.rem(me + (label - BACK) + devs, devs)
         return pltpu.make_async_remote_copy(
             src_ref=bucket.at[part], dst_ref=arrived.at[part],
@@ -151,8 +166,8 @@
 
     greet(me, devs, cores)
     others = [label for label in range(PEERS) if label != BACK]
-    for label in others:
-        copy(label).start()
+    for step in range(PEERS - 1):
+        copy(label_of(ahead(me, jnp.int32(step), devs), me, devs)).start()
     part = pl.ds(BACK * span, span)
     local = pltpu.make_async_copy(bucket.at[part], arrived.at[part], ls)
     local.start()
@@ -228,7 +243,7 @@
         keys[h] = jnp.where(rows_of == h, turned, 0.0).astype(bf16)
         values[h, :, :channels] = jnp.where(lanes_of == h, vals, 0.0).astype(bf16)
         values[h, :, channels:] = jnp.where(lanes_of == h, 1.0, 0.0).astype(bf16)
-    block = 256
+    block = 1024
 
     def row_block(b, carry):
         part = pl.ds(pl.multiple_of(b * block, block), block)

time: 67 us -> 64.1 us (0.957)
  Pallas kernels: 61.9 us -> 58.9 us
    pallas_call x1, Pallas kernels: 19.1 us -> 16.3 us  [per_device(): pl.pallas_call(patch_kernel, out_shape=jax.ShapeDtypeStruct((rows, channe...]
where the time goes in v3:
time: 64.1 us; the launch traced here: 63.8 us
  Pallas kernels  58.9 us (92%)
  local copies, waits for them, and re-layouts  4.68 us (7%)
    pallas_call x1, Pallas kernels, per_device(): pl.pallas_call(functools.partial(swap_kernel, devs, cores), out_shape=jax...  16.4 us
    pallas_call x1, Pallas kernels, per_device(): pl.pallas_call(patch_kernel, out_shape=jax.ShapeDtypeStruct((rows, channe...  16.3 us
    pallas_call x1, Pallas kernels, per_device(): pl.pallas_call(conv_kernel, out_shape=jax.ShapeDtypeStruct((slot_count *...  15.1 us
    pallas_call x1, Pallas kernels, per_device(): pl.pallas_call(functools.partial(halo_kernel, devs, cores), out_shape=(ja...  11.1 us
    unnamed x38, local copies, waits for them, and re-layouts  4.49 us

profile of v3, /device:TPU:0, one launch (start us, length us, event | category | flops | bytes accessed | tf_op | source)
XLA Modules:
  0.0 63.8 jit_solution(12316364006778626300)
XLA Ops:
  0.0 0.8 %copy.21 = s32[4,128]{0,1:T(8,128)S(1)} copy(s32[4,128]{1,0:T(4,128)} %param.21) | data formatting | bytes 4096 | tf_op args[3]
  0.8 0.0 copy-done.16
  0.8 0.1 reshape.3
  0.9 0.1 slice_reduce_fusion
  1.0 0.0 copy-start
  1.0 0.9 %copy-done = bf16[1024,128]{1,0:T(8,128)(2,1)S(1)} copy-done((bf16[1024,128]{1,0:T(8,128)(2,1)S(1)}, bf16[1024,128]{1,0:T(8,128)(2,1)}, u32[]{:S(2)}) %copy-start) | copy-done | bytes 262168
  2.0 11.1 %halo.1 = (bf16[512,128]{1,0:T(8,128)(2,1)S(1)}, s32[128,128]{1,0:T(8,128)S(1)}, s32[1,64]{1,0:T(1,128)S(1)}) custom-call(bf16[1024,128]{1,0:T(8,128)(2,1)S(1)} %copy-done, s32[128,4]{1,0:T(8,128)S(1)} %bitcast.7, s32[64,1]{1,0:T(8,128)S(1)} %get-tuple-element.12.ucol, s32[1,64]{1,0:T(1,128)S(1)} %bitcast.9), custom_call_target="tpu_custom_call" | custom-call | tf_op jit(solution)/shard_map/halo/pallas_call | solution.py:283
  13.1 0.0 copy-done.15
  13.1 0.0 copy-start.1
  13.1 0.0 copy-start.6
  13.1 0.2 copy.22.nbr
  13.3 0.0 copy-start.9
  13.4 0.0 copy-start.8
  13.4 0.0 copy-start.11
  13.4 0.0 copy-start.12
  13.4 0.7 %copy-done.1 = bf16[1024,128]{1,0:T(8,128)(2,1)S(1)} copy-done((bf16[1024,128]{1,0:T(8,128)(2,1)S(1)}, bf16[1024,128]{1,0:T(8,128)(2,1)}, u32[]{:S(2)}) %copy-start.1) | copy-done | bytes 262168
  14.1 0.0 copy-done.8
  14.1 0.0 copy-start.2
  14.1 1.2 %copy-done.2 = bf16[27,128,128]{2,1,0:T(8,128)(2,1)S(1)} copy-done((bf16[27,128,128]{2,1,0:T(8,128)(2,1)S(1)}, bf16[27,128,128]{2,1,0:T(8,128)(2,1)}, u32[]{:S(2)}) %copy-start.2) | copy-done | bytes 884760
  15.2 15.1 %conv.1.bucket = bf16[2048,128]{1,0:T(8,128)(2,1)S(1)} custom-call(bf16[1024,128]{1,0:T(8,128)(2,1)S(1)} %copy-done.1, bf16[512,128]{1,0:T(8,128)(2,1)S(1)} %get-tuple-element.9.halo, s32[1024,27]{1,0:T(8,128)S(1)} %copy.22.nbr, s32[1,64]{1,0:T(1,128)S(1)} %get-tuple-element.10.slots, bf16[27,128,128]{2,1,0:T(8,128)(2,1)S(1)} %copy-done.2, ...), custom_call_target="tpu_custom_call" | custom-call | tf_op jit(solution)/shard_map/conv/pallas_call | solution.py:304
  30.3 0.0 copy-start.17
  30.4 0.0 copy-start.3
  30.4 0.0 copy-start.4
  30.4 0.0 copy-start.5
  30.4 0.0 copy-start.7
  30.4 16.4 %swap.1.arrived = bf16[2048,128]{1,0:T(8,128)(2,1)S(1)} custom-call(bf16[2048,128]{1,0:T(8,128)(2,1)S(1)} %conv.1.bucket), custom_call_target="tpu_custom_call" | custom-call | tf_op jit(solution)/shard_map/swap/pallas_call | solution.py:321
  46.8 0.0 copy-start.10
  46.8 0.0 copy-start.13
  46.8 0.0 copy-start.14
  46.9 0.6 copy-done.10
  47.5 0.0 copy-done.14
  47.5 16.3 %patch.1 = bf16[1024,128]{1,0:T(8,128)(2,1)} custom-call(s32[128,128]{1,0:T(8,128)S(1)} %get-tuple-element.8.places, bf16[2048,128]{1,0:T(8,128)(2,1)S(1)} %swap.1.arrived, f32[3,128]{1,0:T(4,128)S(1)} %copy-done.8, f32[3,128]{1,0:T(4,128)S(1)} %copy-done.9, bf16[128,384]{1,0:T(8,128)(2,1)S(1)} %copy-done.5, f32[1,384]{1,0:T(1,128)S(1)} %broadcast_in_dim.20.qkv_b, ...), custom_call_target="tpu_custom_call" | custom-call | tf_op jit(solution)/shard_map/patch/pallas_call | solution.py:333
  (13 shorter events, 0.0 us)
Async XLA Ops:
  0.0 0.8 %copy-start.16 = (s32[1024]{0:T(1024)S(1)}, s32[1024]{0:T(1024)}, u32[]{:S(2)}) copy-start(s32[1024]{0:T(1024)} %param.19) | copy-start | bytes 12292
  1.0 1.0 %copy-start = (bf16[1024,128]{1,0:T(8,128)(2,1)S(1)}, bf16[1024,128]{1,0:T(8,128)(2,1)}, u32[]{:S(2)}) copy-start(bf16[1024,128]{1,0:T(8,128)(2,1)} %feat.3) | copy-start | bytes 786436
  2.0 11.1 %copy-start.15 = (s32[1024,27]{0,1:T(8,128)S(1)}, s32[1024,27]{0,1:T(8,128)}, u32[]{:S(2)}) copy-start(s32[1024,27]{0,1:T(8,128)} %param.20) | copy-start | bytes 331780
  13.1 1.0 %copy-start.1 = (bf16[1024,128]{1,0:T(8,128)(2,1)S(1)}, bf16[1024,128]{1,0:T(8,128)(2,1)}, u32[]{:S(2)}) copy-start(bf16[1024,128]{1,0:T(8,128)(2,1)} %feat.3) | copy-start | bytes 786436
  13.1 0.9 %copy-start.6 = (bf16[128,128]{1,0:T(8,128)(2,1)S(1)}, bf16[128,128]{1,0:T(8,128)(2,1)}, u32[]{:S(2)}) copy-start(bf16[128,128]{1,0:T(8,128)(2,1)} %cpe_w.1) | copy-start | bytes 98308
  13.3 0.7 %copy-start.9 = (f32[3,128]{1,0:T(4,128)S(1)}, f32[3,128]{1,0:T(4,128)}, u32[]{:S(2)}) copy-start(f32[3,128]{1,0:T(4,128)} %shift.3) | copy-start | bytes 4612
  13.4 0.7 %copy-start.8 = (f32[3,128]{1,0:T(4,128)S(1)}, f32[3,128]{1,0:T(4,128)}, u32[]{:S(2)}) copy-start(f32[3,128]{1,0:T(4,128)} %gain.3) | copy-start | bytes 4612
  13.4 0.7 %copy-start.11 = (f32[128]{0:T(128)S(1)}, f32[128]{0:T(128)}, u32[]{:S(2)}) copy-start(f32[128]{0:T(128)} %param.23) | copy-start | bytes 1540
  13.4 0.7 %copy-start.12 = (f32[128]{0:T(128)S(1)}, f32[128]{0:T(128)}, u32[]{:S(2)}) copy-start(f32[128]{0:T(128)} %param.25) | copy-start | bytes 1540
  14.1 1.2 %copy-start.2 = (bf16[27,128,128]{2,1,0:T(8,128)(2,1)S(1)}, bf16[27,128,128]{2,1,0:T(8,128)(2,1)}, u32[]{:S(2)}) copy-start(bf16[27,128,128]{2,1,0:T(8,128)(2,1)} %conv_w.1) | copy-start | bytes 2654212
  30.3 16.5 %copy-start.17 = (f32[384]{0:T(512)S(1)}, f32[384]{0:T(512)}, u32[]{:S(2)}) copy-start(f32[384]{0:T(512)} %param.29) | copy-start | bytes 4612
  30.4 16.5 %copy-start.3 = (bf16[128,512]{1,0:T(8,128)(2,1)S(1)}, bf16[128,512]{1,0:T(8,128)(2,1)}, u32[]{:S(2)}) copy-start(bf16[128,512]{1,0:T(8,128)(2,1)} %fc1_w.1) | copy-start | bytes 393220
  30.4 16.5 %copy-start.4 = (bf16[512,128]{1,0:T(8,128)(2,1)S(1)}, bf16[512,128]{1,0:T(8,128)(2,1)}, u32[]{:S(2)}) copy-start(bf16[512,128]{1,0:T(8,128)(2,1)} %fc2_w.1) | copy-start | bytes 393220
  30.4 16.5 %copy-start.5 = (bf16[128,384]{1,0:T(8,128)(2,1)S(1)}, bf16[128,384]{1,0:T(8,128)(2,1)}, u32[]{:S(2)}) copy-start(bf16[128,384]{1,0:T(8,128)(2,1)} %qkv_w.1) | copy-start | bytes 294916
  30.4 16.5 %copy-start.7 = (bf16[128,128]{1,0:T(8,128)(2,1)S(1)}, bf16[128,128]{1,0:T(8,128)(2,1)}, u32[]{:S(2)}) copy-start(bf16[128,128]{1,0:T(8,128)(2,1)} %proj_w.1) | copy-start | bytes 98308
  46.8 0.7 %copy-start.10 = (f32[512]{0:T(512)S(1)}, f32[512]{0:T(512)}, u32[]{:S(2)}) copy-start(f32[512]{0:T(512)} %param.33) | copy-start | bytes 6148
  46.8 0.7 %copy-start.13 = (f32[128]{0:T(128)S(1)}, f32[128]{0:T(128)}, u32[]{:S(2)}) copy-start(f32[128]{0:T(128)} %param.31) | copy-start | bytes 1540
  46.8 0.7 %copy-start.14 = (f32[128]{0:T(128)S(1)}, f32[128]{0:T(128)}, u32[]{:S(2)}) copy-start(f32[128]{0:T(128)} %param.35) | copy-start | bytes 1540

commit v4 on v3

--- a/solution.py
+++ b/solution.py
@@ -296,7 +296,7 @@
             dma((4,)), dma((4,)), dma((PEERS,)), dma((PEERS,)),
         ],
         compiler_params=pltpu.CompilerParams(
-            collective_id=0, has_side_effects=True, vmem_limit_bytes=limit
+            collective_id=0, has_side_effects=True, vmem_limit_bytes=limit // 6
         ),
         name="halo",
     )(features, send_rows.T, unit_places[:, None], unit_places[None, :])
@@ -325,7 +325,7 @@
         out_specs=VM,
         scratch_shapes=[dma((PEERS,)), dma((PEERS,)), dma],
         compiler_params=pltpu.CompilerParams(
-            collective_id=1, has_side_effects=True, vmem_limit_bytes=limit
+            collective_id=1, has_side_effects=True, vmem_limit_bytes=limit // 6
         ),
         name="swap",
     )(bucket)

time: 64.1 us -> 64.1 us (level)
  no operation moved by 1% of the time
where the time goes in v4:
time: 64.1 us; the launch traced here: 63.8 us
  Pallas kernels  58.9 us (92%)
  local copies, waits for them, and re-layouts  4.68 us (7%)
    pallas_call x1, Pallas kernels, per_device(): pl.pallas_call(functools.partial(swap_kernel, devs, cores), out_shape=jax...  16.4 us
    pallas_call x1, Pallas kernels, per_device(): pl.pallas_call(patch_kernel, out_shape=jax.ShapeDtypeStruct((rows, channe...  16.3 us
    pallas_call x1, Pallas kernels, per_device(): pl.pallas_call(conv_kernel, out_shape=jax.ShapeDtypeStruct((slot_count *...  15.1 us
    pallas_call x1, Pallas kernels, per_device(): pl.pallas_call(functools.partial(halo_kernel, devs, cores), out_shape=(ja...  11.1 us
    unnamed x38, local copies, waits for them, and re-layouts  4.49 us

profile of v4, /device:TPU:0, one launch (start us, length us, event | category | flops | bytes accessed | tf_op | source)
XLA Modules:
  0.0 63.8 jit_solution(14855621031464019890)
XLA Ops:
  0.0 0.8 %copy.21 = s32[4,128]{0,1:T(8,128)S(1)} copy(s32[4,128]{1,0:T(4,128)} %param.21) | data formatting | bytes 4096 | tf_op args[3]
  0.8 0.0 copy-done.16
  0.8 0.1 reshape.3
  0.9 0.1 slice_reduce_fusion
  1.0 0.0 copy-start
  1.0 0.9 %copy-done = bf16[1024,128]{1,0:T(8,128)(2,1)S(1)} copy-done((bf16[1024,128]{1,0:T(8,128)(2,1)S(1)}, bf16[1024,128]{1,0:T(8,128)(2,1)}, u32[]{:S(2)}) %copy-start) | copy-done | bytes 262168
  2.0 11.1 %halo.1 = (bf16[512,128]{1,0:T(8,128)(2,1)S(1)}, s32[128,128]{1,0:T(8,128)S(1)}, s32[1,64]{1,0:T(1,128)S(1)}) custom-call(bf16[1024,128]{1,0:T(8,128)(2,1)S(1)} %copy-done, s32[128,4]{1,0:T(8,128)S(1)} %bitcast.7, s32[64,1]{1,0:T(8,128)S(1)} %get-tuple-element.12.ucol, s32[1,64]{1,0:T(1,128)S(1)} %bitcast.9), custom_call_target="tpu_custom_call" | custom-call | tf_op jit(solution)/shard_map/halo/pallas_call | solution.py:283
  13.1 0.0 copy-done.15
  13.1 0.0 copy-start.1
  13.1 0.0 copy-start.6
  13.1 0.2 copy.22.nbr
  13.3 0.0 copy-start.9
  13.4 0.0 copy-start.8
  13.4 0.0 copy-start.11
  13.4 0.0 copy-start.12
  13.4 0.7 %copy-done.1 = bf16[1024,128]{1,0:T(8,128)(2,1)S(1)} copy-done((bf16[1024,128]{1,0:T(8,128)(2,1)S(1)}, bf16[1024,128]{1,0:T(8,128)(2,1)}, u32[]{:S(2)}) %copy-start.1) | copy-done | bytes 262168
  14.1 0.0 copy-done.8
  14.1 0.0 copy-start.2
  14.1 1.2 %copy-done.2 = bf16[27,128,128]{2,1,0:T(8,128)(2,1)S(1)} copy-done((bf16[27,128,128]{2,1,0:T(8,128)(2,1)S(1)}, bf16[27,128,128]{2,1,0:T(8,128)(2,1)}, u32[]{:S(2)}) %copy-start.2) | copy-done | bytes 884760
  15.2 15.1 %conv.1.bucket = bf16[2048,128]{1,0:T(8,128)(2,1)S(1)} custom-call(bf16[1024,128]{1,0:T(8,128)(2,1)S(1)} %copy-done.1, bf16[512,128]{1,0:T(8,128)(2,1)S(1)} %get-tuple-element.9.halo, s32[1024,27]{1,0:T(8,128)S(1)} %copy.22.nbr, s32[1,64]{1,0:T(1,128)S(1)} %get-tuple-element.10.slots, bf16[27,128,128]{2,1,0:T(8,128)(2,1)S(1)} %copy-done.2, ...), custom_call_target="tpu_custom_call" | custom-call | tf_op jit(solution)/shard_map/conv/pallas_call | solution.py:304
  30.3 0.0 copy-start.17
  30.4 0.0 copy-start.3
  30.4 0.0 copy-start.4
  30.4 0.0 copy-start.5
  30.4 0.0 copy-start.7
  30.4 16.4 %swap.1.arrived = bf16[2048,128]{1,0:T(8,128)(2,1)S(1)} custom-call(bf16[2048,128]{1,0:T(8,128)(2,1)S(1)} %conv.1.bucket), custom_call_target="tpu_custom_call" | custom-call | tf_op jit(solution)/shard_map/swap/pallas_call | solution.py:321
  46.8 0.0 copy-start.10
  46.8 0.0 copy-start.13
  46.8 0.0 copy-start.14
  46.9 0.6 copy-done.10
  47.5 0.0 copy-done.14
  47.5 16.3 %patch.1 = bf16[1024,128]{1,0:T(8,128)(2,1)} custom-call(s32[128,128]{1,0:T(8,128)S(1)} %get-tuple-element.8.places, bf16[2048,128]{1,0:T(8,128)(2,1)S(1)} %swap.1.arrived, f32[3,128]{1,0:T(4,128)S(1)} %copy-done.8, f32[3,128]{1,0:T(4,128)S(1)} %copy-done.9, bf16[128,384]{1,0:T(8,128)(2,1)S(1)} %copy-done.5, f32[1,384]{1,0:T(1,128)S(1)} %broadcast_in_dim.20.qkv_b, ...), custom_call_target="tpu_custom_call" | custom-call | tf_op jit(solution)/shard_map/patch/pallas_call | solution.py:333
  (13 shorter events, 0.0 us)
Async XLA Ops:
  0.0 0.8 %copy-start.16 = (s32[1024]{0:T(1024)S(1)}, s32[1024]{0:T(1024)}, u32[]{:S(2)}) copy-start(s32[1024]{0:T(1024)} %param.19) | copy-start | bytes 12292
  1.0 1.0 %copy-start = (bf16[1024,128]{1,0:T(8,128)(2,1)S(1)}, bf16[1024,128]{1,0:T(8,128)(2,1)}, u32[]{:S(2)}) copy-start(bf16[1024,128]{1,0:T(8,128)(2,1)} %feat.3) | copy-start | bytes 786436
  2.0 11.1 %copy-start.15 = (s32[1024,27]{0,1:T(8,128)S(1)}, s32[1024,27]{0,1:T(8,128)}, u32[]{:S(2)}) copy-start(s32[1024,27]{0,1:T(8,128)} %param.20) | copy-start | bytes 331780
  13.1 1.0 %copy-start.1 = (bf16[1024,128]{1,0:T(8,128)(2,1)S(1)}, bf16[1024,128]{1,0:T(8,128)(2,1)}, u32[]{:S(2)}) copy-start(bf16[1024,128]{1,0:T(8,128)(2,1)} %feat.3) | copy-start | bytes 786436
  13.1 0.9 %copy-start.6 = (bf16[128,128]{1,0:T(8,128)(2,1)S(1)}, bf16[128,128]{1,0:T(8,128)(2,1)}, u32[]{:S(2)}) copy-start(bf16[128,128]{1,0:T(8,128)(2,1)} %cpe_w.1) | copy-start | bytes 98308
  13.3 0.7 %copy-start.9 = (f32[3,128]{1,0:T(4,128)S(1)}, f32[3,128]{1,0:T(4,128)}, u32[]{:S(2)}) copy-start(f32[3,128]{1,0:T(4,128)} %shift.3) | copy-start | bytes 4612
  13.4 0.7 %copy-start.8 = (f32[3,128]{1,0:T(4,128)S(1)}, f32[3,128]{1,0:T(4,128)}, u32[]{:S(2)}) copy-start(f32[3,128]{1,0:T(4,128)} %gain.3) | copy-start | bytes 4612
  13.4 0.7 %copy-start.11 = (f32[128]{0:T(128)S(1)}, f32[128]{0:T(128)}, u32[]{:S(2)}) copy-start(f32[128]{0:T(128)} %param.23) | copy-start | bytes 1540
  13.4 0.7 %copy-start.12 = (f32[128]{0:T(128)S(1)}, f32[128]{0:T(128)}, u32[]{:S(2)}) copy-start(f32[128]{0:T(128)} %param.25) | copy-start | bytes 1540
  14.1 1.2 %copy-start.2 = (bf16[27,128,128]{2,1,0:T(8,128)(2,1)S(1)}, bf16[27,128,128]{2,1,0:T(8,128)(2,1)}, u32[]{:S(2)}) copy-start(bf16[27,128,128]{2,1,0:T(8,128)(2,1)} %conv_w.1) | copy-start | bytes 2654212
  30.3 16.5 %copy-start.17 = (f32[384]{0:T(512)S(1)}, f32[384]{0:T(512)}, u32[]{:S(2)}) copy-start(f32[384]{0:T(512)} %param.29) | copy-start | bytes 4612
  30.4 16.5 %copy-start.3 = (bf16[128,512]{1,0:T(8,128)(2,1)S(1)}, bf16[128,512]{1,0:T(8,128)(2,1)}, u32[]{:S(2)}) copy-start(bf16[128,512]{1,0:T(8,128)(2,1)} %fc1_w.1) | copy-start | bytes 393220
  30.4 16.5 %copy-start.4 = (bf16[512,128]{1,0:T(8,128)(2,1)S(1)}, bf16[512,128]{1,0:T(8,128)(2,1)}, u32[]{:S(2)}) copy-start(bf16[512,128]{1,0:T(8,128)(2,1)} %fc2_w.1) | copy-start | bytes 393220
  30.4 16.5 %copy-start.5 = (bf16[128,384]{1,0:T(8,128)(2,1)S(1)}, bf16[128,384]{1,0:T(8,128)(2,1)}, u32[]{:S(2)}) copy-start(bf16[128,384]{1,0:T(8,128)(2,1)} %qkv_w.1) | copy-start | bytes 294916
  30.4 16.5 %copy-start.7 = (bf16[128,128]{1,0:T(8,128)(2,1)S(1)}, bf16[128,128]{1,0:T(8,128)(2,1)}, u32[]{:S(2)}) copy-start(bf16[128,128]{1,0:T(8,128)(2,1)} %proj_w.1) | copy-start | bytes 98308
  46.8 0.7 %copy-start.10 = (f32[512]{0:T(512)S(1)}, f32[512]{0:T(512)}, u32[]{:S(2)}) copy-start(f32[512]{0:T(512)} %param.33) | copy-start | bytes 6148
  46.8 0.7 %copy-start.13 = (f32[128]{0:T(128)S(1)}, f32[128]{0:T(128)}, u32[]{:S(2)}) copy-start(f32[128]{0:T(128)} %param.31) | copy-start | bytes 1540
  46.8 0.7 %copy-start.14 = (f32[128]{0:T(128)S(1)}, f32[128]{0:T(128)}, u32[]{:S(2)}) copy-start(f32[128]{0:T(128)} %param.35) | copy-start | bytes 1540
